TPU v7x, 32 devices: a whole 2x2x4 slice. The times are simulated.
32 devices in a mesh: seg: 8 (over z, y), grp: 4 (over x, core).
Axes of the slice: x: 2, y: 2, z: 4, core: 2. Of those that a mesh axis runs over, the one named last changes fastest.
Arguments:
- tokens: bfloat16 [16384, 1024], P(('seg', 'grp')), may hold values from -72 to 72
- w_qkv: bfloat16 [1024, 3072], replicated, may hold values from -0.1875 to 0.1875
- w_out: bfloat16 [1024, 1024], replicated, may hold values from -0.1875 to 0.1875
- block_table: int32 [256, 13], P('seg'), may hold values from 0 to 255, as said below
Outputs:
- mixed: bfloat16 [16384, 1024], P(('seg', 'grp'))
Inputs may be any that keep to these rules, and one draw needn't show every extreme that they name: `block_table`: with segment s of block b = b // 32: column 0 is b; columns 1 to 9 are distinct other blocks of segment s; column 10 + j (j = 0, 1, 2) lies in segment s xor 2**j, and over the 32 query blocks of one segment it names each block of that partner segment once.
All inputs are finite; a program needn't handle non-finite values.
Results may differ from a plain program's by a relative error of at most 0.003.
The roundings to bfloat16 on the way count: a program that leaves them out, or rounds other values in their place, can miss the bound.
Values may be sent and summed in bfloat16 or wider, within the bound.
A program may use at most 128 MiB of HBM per device.

v0:
```python
import jax
import jax.numpy as jnp
from jax import lax
from jax.sharding import PartitionSpec as P

H = 32
HD = 32
BLK = 64
KB = 13


def partner(value, axis, distance):
    mask = 2**distance
    pairs = [(source, source ^ mask) for source in range(lax.axis_size(axis))]
    return lax.ppermute(value, axis, pairs)


def attend(query, pair_rows, block_table, group_size):
    block_count = query.shape[0]
    head_count = query.shape[2]
    group_count = block_count // group_size
    score_scale = HD ** (-0.5)
    query_grp = query.reshape(group_count, group_size, BLK, head_count, HD)
    table_grp = block_table.reshape(group_count, group_size, KB)

    def one_group(payload):
        query_blk, table_blk = payload
        picked = jnp.take(pair_rows, table_blk.reshape(group_size * KB), axis=0)
        picked = picked.reshape(group_size, KB * BLK, 2, head_count, HD)
        key_blk = picked[:, :, 0]
        value_blk = picked[:, :, 1]
        scores = (
            jnp.einsum("gthd,gkhd->ghtk", query_blk, key_blk, preferred_element_type=jnp.float32)
            * score_scale
        )
        row_max = jnp.max(scores, axis=-1, keepdims=True)
        exp_scores = jnp.exp(scores - row_max)
        row_total = jnp.sum(exp_scores, axis=-1, keepdims=True)
        weights = exp_scores.astype(jnp.bfloat16)
        result = jnp.einsum(
            "ghtk,gkhd->gthd", weights, value_blk, preferred_element_type=jnp.float32
        )
        result = result / jnp.transpose(row_total, (0, 2, 1, 3))
        return result.astype(jnp.bfloat16)

    mapped = lax.map(one_group, (query_grp, table_grp))
    return mapped.reshape(block_count * BLK, head_count * HD)


def per_device(tokens, w_qkv, w_out, block_table):
    groups = lax.axis_size("grp")
    heads_dev = H // groups
    lane_count = heads_dev * HD
    tok_rows = tokens.shape[0]
    seg_rows = tok_rows * groups
    seg_blocks = seg_rows // BLK
    row_width = BLK * 2 * lane_count
    projected = jnp.dot(tokens, w_qkv, preferred_element_type=jnp.float32).astype(jnp.bfloat16)
    projected = projected.reshape(tok_rows, 3, groups, lane_count)
    bit_order = (0, 1, 2)
    fetched = {}
    received = lax.all_to_all(projected, "grp", split_axis=2, concat_axis=0, tiled=True).reshape(
        seg_rows, 3, lane_count
    )
    query = received[:, 0]
    own_pairs = received[:, 1:3].reshape(seg_blocks, row_width)
    for bit_place in bit_order:
        fetched[bit_place] = partner(own_pairs, "seg", bit_place)
    pieces = [own_pairs] + [fetched[bit_place] for bit_place in (0, 1, 2)]
    pair_rows = jnp.concatenate(pieces, axis=0)
    group_size = min(seg_blocks, max(1, 512 // BLK))
    segment = lax.axis_index("seg")
    owner_seg = block_table // seg_blocks
    local_block = block_table % seg_blocks
    slot_of = jnp.where(
        owner_seg == segment,
        0,
        jnp.where(
            owner_seg == jnp.bitwise_xor(segment, 1),
            1,
            jnp.where(owner_seg == jnp.bitwise_xor(segment, 2), 2, 3),
        ),
    )
    block_index = slot_of * seg_blocks + local_block
    attended = attend(
        query.reshape(seg_blocks, BLK, heads_dev, HD), pair_rows, block_index, group_size
    )
    mixed_heads = lax.all_to_all(attended, "grp", split_axis=0, concat_axis=1, tiled=True)
    return jnp.dot(mixed_heads, w_out, preferred_element_type=jnp.float32).astype(jnp.bfloat16)


def solution(mesh):
    return jax.shard_map(
        per_device,
        mesh=mesh,
        in_specs=(P(("seg", "grp"), None), P(), P(), P("seg", None)),
        out_specs=P(("seg", "grp"), None),
        check_vma=False,
    )
```

profile of v0, /device:TPU:0, one launch (start us, length us, event | category | flops | bytes accessed | tf_op | source)
XLA Modules:
  0.0 565.3 jit_solution(11662543016315882956)
XLA Ops:
  0.0 8.3 %convolution_convert_fusion = bf16[512,3072]{1,0:T(8,128)(2,1)} fusion(bf16[512,1024]{1,0:T(8,128)(2,1)} %param.6, bf16[1024,3072]{1,0:T(8,128)(2,1)} %param.7), kind=kOutput, calls=%fused_computation.26 | convolution fusion | flops 3222798336 | bytes 10485760 | tf_op jit(solution)/shard_map/dot_general | solution.py:58
  8.3 6.6 %reshape.65 = bf16[512,3,4,256]{3,2,1,0:T(4,128)(2,1)} reshape(bf16[512,3072]{1,0:T(8,128)(2,1)} %convolution_convert_fusion) | data formatting | bytes 6291456 | tf_op jit(solution)/shard_map/reshape | solution.py:59
  17.3 40.9 %all_to_all.34 = bf16[512,3,4,256]{3,0,1,2:T(8,128)(2,1)S(1)} all-to-all(bf16[512,3,4,256]{3,0,1,2:T(8,128)(2,1)S(1)} %copy.21), channel_id=1, replica_groups=mesh['seg'=8,'grp'=4] {'grp'}, dimensions={2} | all-to-all | bytes 6291456 | tf_op jit(solution)/shard_map/all_to_all | solution.py:62
  60.3 14.0 %copy.23 = bf16[2048,2,256]{2,1,0:T(2,128)(2,1)} copy(bf16[2048,2,256]{2,0,1:T(8,128)(2,1)S(1)} %slice.18) | data formatting | bytes 4194304 | tf_op jit(solution)/shard_map/slice | solution.py:66
  74.3 4.5 reshape.67
  91.5 34.6 %collective-permute-done = bf16[32,32768]{1,0:T(8,128)(2,1)} collective-permute-done((bf16[32,32768]{1,0:T(8,128)(2,1)}, bf16[32,32768]{1,0:T(8,128)(2,1)}, u32[]{:S(2)}, u32[]{:S(2)}) %collective-permute-start) | collective-permute-done | bytes 2097184 | tf_op jit(solution)/shard_map/ppermute | solution.py:15
  126.1 46.1 %collective-permute-done.1 = bf16[32,32768]{1,0:T(8,128)(2,1)} collective-permute-done((bf16[32,32768]{1,0:T(8,128)(2,1)}, bf16[32,32768]{1,0:T(8,128)(2,1)}, u32[]{:S(2)}, u32[]{:S(2)}) %collective-permute-start.1) | collective-permute-done | bytes 2097184 | tf_op jit(solution)/shard_map/ppermute | solution.py:15
  174.6 7.0 %pad_maximum_fusion = bf16[128,32768]{1,0:T(8,128)(2,1)} fusion(bf16[32,32768]{1,0:T(8,128)(2,1)} %collective-permute-done.2, bf16[32,32768]{1,0:T(8,128)(2,1)} %collective-permute-done.1, bf16[32,32768]{1,0:T(8,128)(2,1)} %collective-permute-done, bf16[32,32768]{1,0:T(8,128)(2,1)} %reshape.67), kind=kLoop, calls=%fused_computation.25 | loop fusion | flops 33554432 | bytes 16777216 | tf_op jit(solution)/shard_map/concatenate | solution.py:70
  181.6 361.4 %while.10 = (s32[]{:T(128)}, bf16[4,8,64,8,32]{2,1,4,3,0:T(8,128)(2,1)}, s32[4,8,13]{2,1,0:T(8,128)S(1)}, bf16[128,32768]{1,0:T(8,128)(2,1)}, bf16[4,8,64,8,32]{2,1,0,4,3:T(8,128)(2,1)}, /*index=5*/s32[]{:T(128)}) while((s32[]{:T(128)}, bf16[4,8,64,8,32]{2,1,4,3,0:T(8,128)(2,1)}, s32[4,8,13]{2,1,0:T(8,128)S(1)}, bf16[128,32768]{1,0:T(8,128)(2,1)}, ...), condition=%wide.region_3.4_spmd, body=%wide.region_0.3_spmd.sunk | while | flops 467134400 | bytes 187811936 | solution.py:46
  181.7 17.9 %gather_fusion = bf16[104,32768]{1,0:T(8,128)(2,1)} fusion(bf16[128,32768]{1,0:T(8,128)(2,1)} %get-tuple-element.116, s32[1024]{0:T(1024)S(1)} %pad_clamp_fusion.2), kind=kCustom, calls=%fused_computation.clone.1 | custom fusion | bytes 13631904 | tf_op jit(solution)/shard_map/while/body/eval_jaxpr/jit(_take)/gather | solution.py:28
  199.6 22.2 %gather.11 = bf16[8,832,2,8,32]{4,3,2,1,0:T(8,128)(2,1)} reshape(bf16[104,32768]{1,0:T(8,128)(2,1)} %gather_fusion) | data formatting | bytes 13631488 | tf_op jit(solution)/shard_map/while/body/eval_jaxpr/jit(_take)/gather | solution.py:28
  221.8 26.8 %copy.40 = bf16[8,832,2,8,32]{1,4,3,0,2:T(8,128)(2,1)} copy(bf16[8,832,2,8,32]{4,3,2,1,0:T(8,128)(2,1)} %gather.11) | data formatting | bytes 13631488 | tf_op jit(solution)/shard_map/while/body/eval_jaxpr/jit(_take)/gather | solution.py:28
  248.8 4.0 broadcast_select_fusion.2
  256.6 3.4 fusion.29
  261.8 9.0 %fusion.30 = bf16[1,8,64,8,32]{2,4,3,1,0:T(8,128)(2,1)S(1)} fusion(f32[8,8,64,832]{3,2,1,0:T(8,128)} %copy-done.1, f32[8,8,64]{2,1,0:T(8,128)S(1)} %get-tuple-element.100, bf16[8,832,2,8,32]{1,4,3,0,2:T(8,128)(2,1)} %copy-done.2, f32[8,64,8]{1,2,0:T(8,128)S(1)} %bitcast.76), kind=kOutput, calls=%fused_computation.14.clone.1 | convolution fusion | flops 228589568 | bytes 18644992 | tf_op jit(solution)/shard_map/while/body/eval_jaxpr/ghtk,gkhd->gthd/dot_general | solution.py:40
  272.0 17.9 %gather_fusion = bf16[104,32768]{1,0:T(8,128)(2,1)} fusion(bf16[128,32768]{1,0:T(8,128)(2,1)} %get-tuple-element.116, s32[1024]{0:T(1024)S(1)} %pad_clamp_fusion.2), kind=kCustom, calls=%fused_computation.clone.1 | custom fusion | bytes 13631904 | tf_op jit(solution)/shard_map/while/body/eval_jaxpr/jit(_take)/gather | solution.py:28
  289.9 22.2 %gather.11 = bf16[8,832,2,8,32]{4,3,2,1,0:T(8,128)(2,1)} reshape(bf16[104,32768]{1,0:T(8,128)(2,1)} %gather_fusion) | data formatting | bytes 13631488 | tf_op jit(solution)/shard_map/while/body/eval_jaxpr/jit(_take)/gather | solution.py:28
  312.1 26.8 %copy.40 = bf16[8,832,2,8,32]{1,4,3,0,2:T(8,128)(2,1)} copy(bf16[8,832,2,8,32]{4,3,2,1,0:T(8,128)(2,1)} %gather.11) | data formatting | bytes 13631488 | tf_op jit(solution)/shard_map/while/body/eval_jaxpr/jit(_take)/gather | solution.py:28
  339.1 4.0 broadcast_select_fusion.2
  346.9 3.4 fusion.29
  352.1 9.0 %fusion.30 = bf16[1,8,64,8,32]{2,4,3,1,0:T(8,128)(2,1)S(1)} fusion(f32[8,8,64,832]{3,2,1,0:T(8,128)} %copy-done.1, f32[8,8,64]{2,1,0:T(8,128)S(1)} %get-tuple-element.100, bf16[8,832,2,8,32]{1,4,3,0,2:T(8,128)(2,1)} %copy-done.2, f32[8,64,8]{1,2,0:T(8,128)S(1)} %bitcast.76), kind=kOutput, calls=%fused_computation.14.clone.1 | convolution fusion | flops 228589568 | bytes 18644992 | tf_op jit(solution)/shard_map/while/body/eval_jaxpr/ghtk,gkhd->gthd/dot_general | solution.py:40
  362.3 17.9 %gather_fusion = bf16[104,32768]{1,0:T(8,128)(2,1)} fusion(bf16[128,32768]{1,0:T(8,128)(2,1)} %get-tuple-element.116, s32[1024]{0:T(1024)S(1)} %pad_clamp_fusion.2), kind=kCustom, calls=%fused_computation.clone.1 | custom fusion | bytes 13631904 | tf_op jit(solution)/shard_map/while/body/eval_jaxpr/jit(_take)/gather | solution.py:28
  380.2 22.2 %gather.11 = bf16[8,832,2,8,32]{4,3,2,1,0:T(8,128)(2,1)} reshape(bf16[104,32768]{1,0:T(8,128)(2,1)} %gather_fusion) | data formatting | bytes 13631488 | tf_op jit(solution)/shard_map/while/body/eval_jaxpr/jit(_take)/gather | solution.py:28
  402.4 26.8 %copy.40 = bf16[8,832,2,8,32]{1,4,3,0,2:T(8,128)(2,1)} copy(bf16[8,832,2,8,32]{4,3,2,1,0:T(8,128)(2,1)} %gather.11) | data formatting | bytes 13631488 | tf_op jit(solution)/shard_map/while/body/eval_jaxpr/jit(_take)/gather | solution.py:28
  429.5 4.0 broadcast_select_fusion.2
  442.4 9.0 %fusion.30 = bf16[1,8,64,8,32]{2,4,3,1,0:T(8,128)(2,1)S(1)} fusion(f32[8,8,64,832]{3,2,1,0:T(8,128)} %copy-done.1, f32[8,8,64]{2,1,0:T(8,128)S(1)} %get-tuple-element.100, bf16[8,832,2,8,32]{1,4,3,0,2:T(8,128)(2,1)} %copy-done.2, f32[8,64,8]{1,2,0:T(8,128)S(1)} %bitcast.76), kind=kOutput, calls=%fused_computation.14.clone.1 | convolution fusion | flops 228589568 | bytes 18644992 | tf_op jit(solution)/shard_map/while/body/eval_jaxpr/ghtk,gkhd->gthd/dot_general | solution.py:40
  452.7 17.9 %gather_fusion = bf16[104,32768]{1,0:T(8,128)(2,1)} fusion(bf16[128,32768]{1,0:T(8,128)(2,1)} %get-tuple-element.116, s32[1024]{0:T(1024)S(1)} %pad_clamp_fusion.2), kind=kCustom, calls=%fused_computation.clone.1 | custom fusion | bytes 13631904 | tf_op jit(solution)/shard_map/while/body/eval_jaxpr/jit(_take)/gather | solution.py:28
  470.6 22.2 %gather.11 = bf16[8,832,2,8,32]{4,3,2,1,0:T(8,128)(2,1)} reshape(bf16[104,32768]{1,0:T(8,128)(2,1)} %gather_fusion) | data formatting | bytes 13631488 | tf_op jit(solution)/shard_map/while/body/eval_jaxpr/jit(_take)/gather | solution.py:28
  492.8 26.8 %copy.40 = bf16[8,832,2,8,32]{1,4,3,0,2:T(8,128)(2,1)} copy(bf16[8,832,2,8,32]{4,3,2,1,0:T(8,128)(2,1)} %gather.11) | data formatting | bytes 13631488 | tf_op jit(solution)/shard_map/while/body/eval_jaxpr/jit(_take)/gather | solution.py:28
  519.8 4.0 broadcast_select_fusion.2
  532.8 9.0 %fusion.30 = bf16[1,8,64,8,32]{2,4,3,1,0:T(8,128)(2,1)S(1)} fusion(f32[8,8,64,832]{3,2,1,0:T(8,128)} %copy-done.1, f32[8,8,64]{2,1,0:T(8,128)S(1)} %get-tuple-element.100, bf16[8,832,2,8,32]{1,4,3,0,2:T(8,128)(2,1)} %copy-done.2, f32[8,64,8]{1,2,0:T(8,128)S(1)} %bitcast.76), kind=kOutput, calls=%fused_computation.14.clone.1 | convolution fusion | flops 228589568 | bytes 18644992 | tf_op jit(solution)/shard_map/while/body/eval_jaxpr/ghtk,gkhd->gthd/dot_general | solution.py:40
  546.1 16.9 %all_to_all.35 = bf16[4,512,256]{1,2,0:T(8,128)(2,1)S(1)} all-to-all(bf16[4,512,256]{1,2,0:T(8,128)(2,1)S(1)} %all_to_all.28), channel_id=1, replica_groups=mesh['seg'=8,'grp'=4] {'grp'}, dimensions={0} | all-to-all | bytes 2097152 | tf_op jit(solution)/shard_map/all_to_all | solution.py:88
  (75 shorter events, 59.4 us)
Async XLA Ops:
  0.0 563.0 %copy-start = (bf16[1024,1024]{1,0:T(8,128)(2,1)S(1)}, bf16[1024,1024]{1,0:T(8,128)(2,1)}, u32[]{:S(2)}) copy-start(bf16[1024,1024]{1,0:T(8,128)(2,1)} %param.8) | copy-start | bytes 6291460
  58.5 1.7 copy-start.3
  58.5 26.0 %copy-start.4 = (s32[32,13]{0,1:T(8,128)S(1)}, s32[32,13]{0,1:T(8,128)}, u32[]{:S(2)}) copy-start(s32[32,13]{0,1:T(8,128)} %param.9) | copy-start | bytes 4996
  78.8 47.3 %collective-permute-start = (bf16[32,32768]{1,0:T(8,128)(2,1)}, bf16[32,32768]{1,0:T(8,128)(2,1)}, u32[]{:S(2)}, u32[]{:S(2)}) collective-permute-start(bf16[32,32768]{1,0:T(8,128)(2,1)} %reshape.67), channel_id=1, source_target_pairs={{0,4},{4,0},{8,12},{12,8},{16,20},{20,16},{24,28},{28,24},{1,5},{5... | collective-permute-start | bytes 6291464 | tf_op jit(solution)/shard_map/ppermute | solution.py:15
  80.3 91.8 %collective-permute-start.1 = (bf16[32,32768]{1,0:T(8,128)(2,1)}, bf16[32,32768]{1,0:T(8,128)(2,1)}, u32[]{:S(2)}, u32[]{:S(2)}) collective-permute-start(bf16[32,32768]{1,0:T(8,128)(2,1)} %reshape.67), channel_id=1, source_target_pairs={{0,8},{4,12},{8,0},{12,4},{16,24},{20,28},{24,16},{28,20},{1,9},{5... | collective-permute-start | bytes 6291464 | tf_op jit(solution)/shard_map/ppermute | solution.py:15
  81.9 92.7 %collective-permute-start.2 = (bf16[32,32768]{1,0:T(8,128)(2,1)}, bf16[32,32768]{1,0:T(8,128)(2,1)}, u32[]{:S(2)}, u32[]{:S(2)}) collective-permute-start(bf16[32,32768]{1,0:T(8,128)(2,1)} %reshape.67), channel_id=1, source_target_pairs={{0,16},{4,20},{8,24},{12,28},{16,0},{20,4},{24,8},{28,12},{1,17},{... | collective-permute-start | bytes 6291464 | tf_op jit(solution)/shard_map/ppermute | solution.py:15
  252.8 3.8 copy-start.2
  256.6 5.2 copy-start.1
  343.1 3.8 copy-start.2
  346.9 5.2 copy-start.1
  433.5 3.8 copy-start.2
  437.2 5.2 copy-start.1
  523.8 3.8 copy-start.2
  527.6 5.2 copy-start.1
where the time goes:
time: 569 us; the launch traced here: 565 us
  local copies, waits for them, and re-layouts  326 us (57%)
  waiting for transfers between devices  83 us (15%)
  blocking collectives  57.8 us (10%)
  matrix products  55.5 us (10%)
  other arithmetic  36.8 us (6%)
  starting transfers between devices  5.69 us (1%)
    gather x12, local copies, waits for them, and re-layouts, one_group(): picked = jnp.take(pair_rows, table_blk.reshape(group_size * KB), axis=0)  268 us
    ppermute x3, waiting for transfers between devices, partner(): return lax.ppermute(value, axis, pairs)  83 us
    all_to_all x1, blocking collectives, per_device(): lax.all_to_all(projected, 'grp', split_axis=2, concat_axis=0, tiled=True)  40.9 us
    dot_general x4, matrix products, one_group(): jnp.einsum('ghtk,gkhd->gthd', weights, value_blk, preferred_element_type=...  36 us
    all_to_all x1, blocking collectives, per_device(): lax.all_to_all(attended, 'grp', split_axis=0, concat_axis=1, tiled=True)  16.9 us
    select_n x8, other arithmetic, one_group(): picked = jnp.take(pair_rows, table_blk.reshape(group_size * KB), axis=0)  16 us
    slice x2, local copies, waits for them, and re-layouts, per_device(): own_pairs = received[:, 1:3].reshape(seg_blocks, row_width)  14.1 us
    reduce_sum x4, other arithmetic, one_group(): row_total = jnp.sum(exp_scores, axis=-1, keepdims=True)  13.7 us
  transfers between devices with their start and end apart: 3, of which 3 were waited for; matrix products, arithmetic and copies ran while one was open for 1% of the time, Pallas kernels for 0%

commit v1 on v0

v1 whole, which is shorter than its diff:
```python
import functools

import jax
import jax.numpy as jnp
from jax import lax
from jax.experimental import pallas as pl
from jax.experimental.pallas import tpu as pltpu
from jax.sharding import PartitionSpec as P

H = 32
HD = 32
BLK = 64
KB = 13
N_PARTNER = 3
N_OWN = KB - N_PARTNER
LANES = 256
LOG2E = 1.4426950408889634


def exchange(value, axis, mask):
    pairs = [(source, source ^ mask) for source in range(lax.axis_size(axis))]
    return lax.ppermute(value, axis, pairs)


def gather_shards(value, axis):
    held = {0: value}
    mask = lax.axis_size(axis) // 2
    while mask >= 1:
        for k in list(held):
            held[k ^ mask] = exchange(held[k], axis, mask)
        mask //= 2
    return [held[k] for k in range(len(held))]


def pick_body(index_ref, rows_ref, out_ref):
    out_ref[...] = rows_ref[...]


def pick_blocks(rows, index):
    count = index.shape[0]
    width = rows.shape[1]
    return pl.pallas_call(
        pick_body,
        grid_spec=pltpu.PrefetchScalarGridSpec(
            num_scalar_prefetch=1,
            grid=(count,),
            in_specs=[pl.BlockSpec((BLK, width), lambda i, index: (index[i], 0))],
            out_specs=pl.BlockSpec((BLK, width), lambda i, index: (i, 0)),
        ),
        out_shape=jax.ShapeDtypeStruct((count * BLK, width), rows.dtype),
        cost_estimate=pl.CostEstimate(
            flops=0, bytes_accessed=4 * count * BLK * width, transcendentals=0
        ),
    )(index, rows)


def attend_body(index_ref, q_ref, ko_ref, vo_ref, *refs):
    kc_refs = refs[:N_PARTNER]
    vc_refs = refs[N_PARTNER : 2 * N_PARTNER]
    out_ref, k_buf, v_buf = refs[2 * N_PARTNER :]
    block = pl.program_id(1)
    for c in range(N_OWN):
        start = pl.multiple_of(index_ref[block * N_OWN + c] * BLK, BLK)
        k_buf[c * BLK : (c + 1) * BLK, :] = ko_ref[pl.ds(start, BLK), :]
        v_buf[c * BLK : (c + 1) * BLK, :] = vo_ref[pl.ds(start, BLK), :]
    for j in range(N_PARTNER):
        c = N_OWN + j
        k_buf[c * BLK : (c + 1) * BLK, :] = kc_refs[j][...]
        v_buf[c * BLK : (c + 1) * BLK, :] = vc_refs[j][...]
    q = q_ref[...]
    head = lax.broadcasted_iota(jnp.int32, (BLK, LANES), 1) // HD
    heads = LANES // HD
    zero = jnp.zeros_like(q)
    spread = jnp.concatenate([jnp.where(head == h, q, zero) for h in range(heads)], axis=0)
    raw = lax.dot_general(
        spread, k_buf[...], (((1,), (1,)), ((), ())), preferred_element_type=jnp.float32
    )
    factor = HD ** (-0.5) * LOG2E
    top = jnp.max(raw, axis=1, keepdims=True) * factor
    exps = jnp.exp2(raw * factor - top)
    total = jnp.sum(exps, axis=1, keepdims=True)
    result = jnp.dot(
        exps.astype(jnp.bfloat16), v_buf[...], preferred_element_type=jnp.float32
    )
    result = result / total
    out = result[0:BLK]
    for h in range(1, heads):
        out = jnp.where(head == h, result[h * BLK : (h + 1) * BLK], out)
    out_ref[...] = out.astype(jnp.bfloat16)


def attend(index, query, own, crosses):
    rows, width = query.shape
    lane_groups = width // LANES
    blocks = rows // BLK
    own_rows = own.shape[0]
    here = lambda hg, i, index: (i, hg)
    value_here = lambda hg, i, index: (i, lane_groups + hg)
    keys = blocks * KB * BLK
    return pl.pallas_call(
        attend_body,
        grid_spec=pltpu.PrefetchScalarGridSpec(
            num_scalar_prefetch=1,
            grid=(lane_groups, blocks),
            in_specs=[
                pl.BlockSpec((BLK, LANES), here),
                pl.BlockSpec((own_rows, LANES), lambda hg, i, index: (0, hg)),
                pl.BlockSpec((own_rows, LANES), lambda hg, i, index: (0, lane_groups + hg)),
            ]
            + [pl.BlockSpec((BLK, LANES), here)] * N_PARTNER
            + [pl.BlockSpec((BLK, LANES), value_here)] * N_PARTNER,
            out_specs=pl.BlockSpec((BLK, LANES), here),
            scratch_shapes=[pltpu.VMEM((KB * BLK, LANES), jnp.bfloat16)] * 2,
        ),
        out_shape=jax.ShapeDtypeStruct((rows, width), jnp.bfloat16),
        compiler_params=pltpu.CompilerParams(vmem_limit_bytes=48 * 1024 * 1024),
        cost_estimate=pl.CostEstimate(
            flops=4 * BLK * keys * width,
            bytes_accessed=own.size * 2,
            transcendentals=BLK * keys * H,
        ),
    )(index, query, own, own, *crosses, *crosses)


def project(rows, weights):
    return jnp.dot(rows, weights, preferred_element_type=jnp.float32).astype(jnp.bfloat16)


def per_device(tokens, w_qkv, w_out, block_table):
    groups = lax.axis_size("grp")
    me = lax.axis_index("grp")
    tok_rows, width = tokens.shape
    blocks = tok_rows // BLK
    seg_blocks = blocks * groups

    table = lax.dynamic_slice_in_dim(block_table, me * blocks, blocks, axis=0) % seg_blocks
    place = ((table // blocks) ^ me) * blocks + table % blocks
    asked = [exchange(table[:, N_OWN + j], "seg", 1 << j) for j in range(N_PARTNER)]

    shards = gather_shards(tokens, "grp")
    rows = jnp.concatenate(shards, axis=0)
    arrived = []
    for j in reversed(range(N_PARTNER)):
        want = ((asked[j] // blocks) ^ me) * blocks + asked[j] % blocks
        arrived.append(exchange(pick_blocks(rows, want), "seg", 1 << j))
    arrived = arrived[::-1]

    query = project(tokens, w_qkv[:, :width])
    own = project(rows, w_qkv[:, width:])
    crosses = [project(part, w_qkv[:, width:]) for part in arrived]
    attended = attend(place[:, :N_OWN].reshape(-1), query, own, crosses)
    return project(attended, w_out)


def solution(mesh):
    return jax.shard_map(
        per_device,
        mesh=mesh,
        in_specs=(P(("seg", "grp"), None), P(), P(), P("seg", None)),
        out_specs=P(("seg", "grp"), None),
        check_vma=False,
    )
```

time: 569 us -> 163 us (0.29)
  local copies, waits for them, and re-layouts: 326 us -> 6.92 us
  Pallas kernels: 0 us -> 72.2 us
  blocking collectives: 57.8 us -> 0 us
  waiting for transfers between devices: 83 us -> 31.4 us
  other arithmetic: 36.8 us -> 2.41 us
  matrix products: 55.5 us -> 34.5 us
  starting transfers between devices: 5.69 us -> 14.6 us
    gather x12 -> x0, local copies, waits for them, and re-layouts: 268 us -> none  [one_group(): picked = jnp.take(pair_rows, table_blk.reshape(group_size * KB), axis=0)]
    pallas_call x0 -> x4, Pallas kernels: none -> 72.2 us  [the longest x1 54.6 us: attend(): pl.pallas_call(attend_body, grid_spec=pltpu.PrefetchScalarGridSpec(num_sc...]
    all_to_all x2 -> x0, blocking collectives: 57.8 us -> none  [the longest x1 40.9 us: per_device(): lax.all_to_all(projected, 'grp', split_axis=2, concat_axis=0, tiled=True)]
    ppermute x3 -> x9, waiting for transfers between devices: 83 us -> 31.4 us  [exchange(): return lax.ppermute(value, axis, pairs)]
    dot_general x10 -> x6, matrix products: 55.5 us -> 34.5 us  [project(): jnp.dot(rows, weights, preferred_element_type=jnp.float32)]
    slice x4 -> x1, local copies, waits for them, and re-layouts: 17.9 us -> 0.08 us  [per_device(): attended = attend(place[:, :N_OWN].reshape(-1), query, own, crosses)]
    select_n x8 -> x0, other arithmetic: 16 us -> none  [one_group(): picked = jnp.take(pair_rows, table_blk.reshape(group_size * KB), axis=0)]
    reshape x7 -> x1, local copies, waits for them, and re-layouts: 13.8 us -> 0.08 us  [per_device(): attended = attend(place[:, :N_OWN].reshape(-1), query, own, crosses)]
  transfers between devices with their start and end apart: 3 -> 9, of which waited for: 3 -> 2; matrix products, arithmetic and copies ran while one was open for 1% -> 24% of each run, Pallas kernels for 0% -> 7%
where the time goes in v1:
time: 163 us; the launch traced here: 162 us
  Pallas kernels  72.2 us (44%)
  matrix products  34.5 us (21%)
  waiting for transfers between devices  31.4 us (19%)
  starting transfers between devices  14.6 us (9%)
  local copies, waits for them, and re-layouts  6.92 us (4%)
  other arithmetic  2.41 us (1%)
    pallas_call x1, Pallas kernels, attend(): pl.pallas_call(attend_body, grid_spec=pltpu.PrefetchScalarGridSpec(num_sc...  54.6 us
    dot_general x6, matrix products, project(): jnp.dot(rows, weights, preferred_element_type=jnp.float32)  34.5 us
    ppermute x9, waiting for transfers between devices, exchange(): return lax.ppermute(value, axis, pairs)  31.4 us
    pallas_call x3, Pallas kernels, pick_blocks(): pl.pallas_call(pick_body, grid_spec=pltpu.PrefetchScalarGridSpec(num_scal...  17.5 us
    ppermute x9, starting transfers between devices, exchange(): return lax.ppermute(value, axis, pairs)  14.6 us
    unnamed x11, local copies, waits for them, and re-layouts  5.68 us
  transfers between devices with their start and end apart: 9, of which 2 were waited for; matrix products, arithmetic and copies ran while one was open for 24% of the time, Pallas kernels for 7%

profile of v1, /device:TPU:0, one launch (start us, length us, event | category | flops | bytes accessed | tf_op | source)
XLA Modules:
  0.0 162.1 jit_solution(16418825993230562300)
XLA Ops:
  0.0 2.9 %collective-permute-start.1 = (bf16[512,1024]{1,0:T(8,128)(2,1)}, bf16[512,1024]{1,0:T(8,128)(2,1)}, u32[]{:S(2)}, u32[]{:S(2)}) collective-permute-start(bf16[512,1024]{1,0:T(8,128)(2,1)} %param.4), channel_id=1, source_target_pairs={{0,2},{1,3},{2,0},{3,1},{4,6},{5,7},{6,4},{7,5},{8,10},{9,11},{10,... | collective-permute-start | bytes 3145736 | tf_op jit(solution)/shard_map/ppermute | solution.py:22
  2.9 0.0 collective-permute-start
  2.9 0.8 negate_select_fusion
  3.7 2.7 %collective-permute-start.7 = (s32[8]{0:T(128)S(1)}, s32[8]{0:T(128)S(1)}, u32[]{:S(2)}, u32[]{:S(2)}) collective-permute-start(s32[8]{0:T(128)S(1)} %get-tuple-element.7), channel_id=1, source_target_pairs={{0,16},{4,20},{8,24},{12,28},{16,0},{20,4},{24,8},{28,12},{1,17},{... | collective-permute-start | bytes 104 | tf_op jit(solution)/shard_map/ppermute | solution.py:22
  6.4 1.6 collective-permute-start.5
  8.0 1.5 collective-permute-start.3
  9.5 0.1 copy.5
  9.6 0.1 reshape.3.index_ref
  9.7 3.2 %fusion.6.q_ref = bf16[512,1024]{1,0:T(8,128)(2,1)S(1)} fusion(bf16[512,1024]{1,0:T(8,128)(2,1)} %param.4, bf16[1024,3072]{1,0:T(8,128)(2,1)} %param.5), kind=kOutput, calls=%fused_computation.10 | convolution fusion | flops 1074266112 | bytes 4194304 | tf_op jit(solution)/shard_map/dot_general | solution.py:126
  12.9 13.5 %collective-permute-done.1 = bf16[512,1024]{1,0:T(8,128)(2,1)} collective-permute-done((bf16[512,1024]{1,0:T(8,128)(2,1)}, bf16[512,1024]{1,0:T(8,128)(2,1)}, u32[]{:S(2)}, u32[]{:S(2)}) %collective-permute-start.1) | collective-permute-done | bytes 1048608 | tf_op jit(solution)/shard_map/ppermute | solution.py:22
  26.4 0.0 collective-permute-start.2
  26.4 1.1 constant_dynamic-update-slice_fusion.3
  27.5 0.5 fusion.17.index_ref
  28.0 0.5 fusion.16.index_ref
  28.6 0.6 fusion.15.index_ref
  29.2 0.0 collective-permute-done
  29.2 2.3 %constant_dynamic-update-slice_fusion.2 = bf16[2048,1024]{1,0:T(8,128)(2,1)} fusion(bf16[2048,1024]{1,0:T(8,128)(2,1)} %constant_dynamic-update-slice_fusion.3, bf16[512,1024]{1,0:T(8,128)(2,1)} %collective-permute-done), kind=kLoop, calls=%fused_computation.21 | loop fusion | bytes 2097152
  31.4 2.3 %constant_dynamic-update-slice_fusion.1 = bf16[2048,1024]{1,0:T(8,128)(2,1)} fusion(bf16[2048,1024]{1,0:T(8,128)(2,1)} %constant_dynamic-update-slice_fusion.2, bf16[512,1024]{1,0:T(8,128)(2,1)} %collective-permute-done.1), kind=kLoop, calls=%fused_computation.20 | loop fusion | bytes 2097152
  33.7 1.1 constant_dynamic-update-slice_fusion.rows_ref
  34.8 5.8 %shard_map.48 = bf16[512,1024]{1,0:T(8,128)(2,1)} custom-call(s32[8]{0:T(128)} %fusion.17.index_ref, bf16[2048,1024]{1,0:T(8,128)(2,1)} %constant_dynamic-update-slice_fusion.rows_ref), custom_call_target="tpu_custom_call" | custom-call | bytes 2097152 | tf_op jit(solution)/shard_map/pallas_call | solution.py:42
  40.6 2.8 %collective-permute-start.8 = (bf16[512,1024]{1,0:T(8,128)(2,1)}, bf16[512,1024]{1,0:T(8,128)(2,1)}, u32[]{:S(2)}, u32[]{:S(2)}) collective-permute-start(bf16[512,1024]{1,0:T(8,128)(2,1)} %shard_map.48), channel_id=1, source_target_pairs={{0,16},{4,20},{8,24},{12,28},{16,0},{20,4},{24,8},{28,12},{1,17},{... | collective-permute-start | bytes 3145736 | tf_op jit(solution)/shard_map/ppermute | solution.py:22
  43.5 5.8 %shard_map.47 = bf16[512,1024]{1,0:T(8,128)(2,1)} custom-call(s32[8]{0:T(128)} %fusion.16.index_ref, bf16[2048,1024]{1,0:T(8,128)(2,1)} %constant_dynamic-update-slice_fusion.rows_ref), custom_call_target="tpu_custom_call" | custom-call | bytes 2097152 | tf_op jit(solution)/shard_map/pallas_call | solution.py:42
  49.3 1.6 collective-permute-start.6
  50.9 14.0 %convolution_convert_fusion.ko_ref.vo_ref = bf16[2048,2048]{1,0:T(8,128)(2,1)} fusion(bf16[2048,1024]{1,0:T(8,128)(2,1)} %constant_dynamic-update-slice_fusion.rows_ref, bf16[1024,3072]{1,0:T(8,128)(2,1)} %param.5), kind=kOutput, calls=%fused_computation | convolution fusion | flops 8594128896 | bytes 16777216 | tf_op jit(solution)/shard_map/dot_general | solution.py:126
  64.9 5.9 %shard_map.46 = bf16[512,1024]{1,0:T(8,128)(2,1)} custom-call(s32[8]{0:T(128)} %fusion.15.index_ref, bf16[2048,1024]{1,0:T(8,128)(2,1)} %constant_dynamic-update-slice_fusion.rows_ref), custom_call_target="tpu_custom_call" | custom-call | bytes 2097152 | tf_op jit(solution)/shard_map/pallas_call | solution.py:42
  70.8 1.5 collective-permute-start.4
  72.3 17.9 %collective-permute-done.8 = bf16[512,1024]{1,0:T(8,128)(2,1)} collective-permute-done((bf16[512,1024]{1,0:T(8,128)(2,1)}, bf16[512,1024]{1,0:T(8,128)(2,1)}, u32[]{:S(2)}, u32[]{:S(2)}) %collective-permute-start.8) | collective-permute-done | bytes 1048608 | tf_op jit(solution)/shard_map/ppermute | solution.py:22
  90.2 6.4 %convolution_convert_fusion.1.refs_2_.refs_5_ = bf16[512,2048]{1,0:T(8,128)(2,1)} fusion(bf16[512,1024]{1,0:T(8,128)(2,1)} %collective-permute-done.8, bf16[1024,3072]{1,0:T(8,128)(2,1)} %param.5), kind=kOutput, calls=%fused_computation.1 | convolution fusion | flops 2148532224 | bytes 7340032 | tf_op jit(solution)/shard_map/dot_general | solution.py:126
  96.6 6.3 %convolution_convert_fusion.2.refs_1_.refs_4_ = bf16[512,2048]{1,0:T(8,128)(2,1)} fusion(bf16[512,1024]{1,0:T(8,128)(2,1)} %collective-permute-done.6, bf16[1024,3072]{1,0:T(8,128)(2,1)} %param.5), kind=kOutput, calls=%fused_computation.2 | convolution fusion | flops 2148532224 | bytes 7340032 | tf_op jit(solution)/shard_map/dot_general | solution.py:126
  102.9 2.3 %convolution_convert_fusion.3.refs_0_.refs_3_ = bf16[512,2048]{1,0:T(8,128)(2,1)S(1)} fusion(bf16[512,1024]{1,0:T(8,128)(2,1)S(1)} %collective-permute-done.4, bf16[1024,3072]{1,0:T(8,128)(2,1)S(1)} %bitcast.14), kind=kOutput, calls=%fused_computation.3 | convolution fusion | flops 2148532224 | bytes 7340032 | tf_op jit(solution)/shard_map/dot_general | solution.py:126
  105.3 54.6 %shard_map.49 = bf16[512,1024]{1,0:T(8,128)(2,1)S(1)} custom-call(s32[80]{0:T(128)S(1)} %reshape.3.index_ref, bf16[512,1024]{1,0:T(8,128)(2,1)S(1)} %fusion.6.q_ref, bf16[2048,2048]{1,0:T(8,128)(2,1)} %convolution_convert_fusion.ko_ref.vo_ref, bf16[2048,2048]{1,0:T(8,128)(2,1)} %convolution_convert_fusion.ko_ref.vo_ref, ...), custom_call_target="tpu_custom_call" | custom-call | flops 1744830464 | bytes 8388608 | tf_op jit(solution)/shard_map/pallas_call | solution.py:100
  159.9 2.2 %convolution_convert_fusion.4 = bf16[512,1024]{1,0:T(8,128)(2,1)} fusion(bf16[512,1024]{1,0:T(8,128)(2,1)S(1)} %shard_map.49, bf16[1024,1024]{1,0:T(8,128)(2,1)S(1)} %copy-done), kind=kOutput, calls=%fused_computation.11 | convolution fusion | flops 1074266112 | bytes 4194304 | tf_op jit(solution)/shard_map/dot_general | solution.py:126
  (19 shorter events, 0.1 us)
Async XLA Ops:
  0.0 159.9 %copy-start = (bf16[1024,1024]{1,0:T(8,128)(2,1)S(1)}, bf16[1024,1024]{1,0:T(8,128)(2,1)}, u32[]{:S(2)}) copy-start(bf16[1024,1024]{1,0:T(8,128)(2,1)} %param.6) | copy-start | bytes 6291460
  0.0 26.4 %collective-permute-start.1 = (bf16[512,1024]{1,0:T(8,128)(2,1)}, bf16[512,1024]{1,0:T(8,128)(2,1)}, u32[]{:S(2)}, u32[]{:S(2)}) collective-permute-start(bf16[512,1024]{1,0:T(8,128)(2,1)} %param.4), channel_id=1, source_target_pairs={{0,2},{1,3},{2,0},{3,1},{4,6},{5,7},{6,4},{7,5},{8,10},{9,11},{10,... | collective-permute-start | bytes 3145736 | tf_op jit(solution)/shard_map/ppermute | solution.py:22
  2.9 26.2 %collective-permute-start = (bf16[512,1024]{1,0:T(8,128)(2,1)}, bf16[512,1024]{1,0:T(8,128)(2,1)}, u32[]{:S(2)}, u32[]{:S(2)}) collective-permute-start(bf16[512,1024]{1,0:T(8,128)(2,1)} %param.4), channel_id=1, source_target_pairs={{0,1},{1,0},{2,3},{3,2},{4,5},{5,4},{6,7},{7,6},{8,9},{9,8},{10,11... | collective-permute-start | bytes 3145736 | tf_op jit(solution)/shard_map/ppermute | solution.py:22
  3.7 23.8 %collective-permute-start.7 = (s32[8]{0:T(128)S(1)}, s32[8]{0:T(128)S(1)}, u32[]{:S(2)}, u32[]{:S(2)}) collective-permute-start(s32[8]{0:T(128)S(1)} %get-tuple-element.7), channel_id=1, source_target_pairs={{0,16},{4,20},{8,24},{12,28},{16,0},{20,4},{24,8},{28,12},{1,17},{... | collective-permute-start | bytes 104 | tf_op jit(solution)/shard_map/ppermute | solution.py:22
  6.4 21.6 %collective-permute-start.5 = (s32[8]{0:T(128)S(1)}, s32[8]{0:T(128)S(1)}, u32[]{:S(2)}, u32[]{:S(2)}) collective-permute-start(s32[8]{0:T(128)S(1)} %get-tuple-element.8), channel_id=1, source_target_pairs={{0,8},{4,12},{8,0},{12,4},{16,24},{20,28},{24,16},{28,20},{1,9},{5... | collective-permute-start | bytes 104 | tf_op jit(solution)/shard_map/ppermute | solution.py:22
  8.0 20.6 %collective-permute-start.3 = (s32[8]{0:T(128)S(1)}, s32[8]{0:T(128)S(1)}, u32[]{:S(2)}, u32[]{:S(2)}) collective-permute-start(s32[8]{0:T(128)S(1)} %get-tuple-element.9), channel_id=1, source_target_pairs={{0,4},{4,0},{8,12},{12,8},{16,20},{20,16},{24,28},{28,24},{1,5},{5... | collective-permute-start | bytes 104 | tf_op jit(solution)/shard_map/ppermute | solution.py:22
  9.7 16.7 %copy-start.1 = (bf16[512,1024]{1,0:T(8,128)(2,1)S(1)}, bf16[512,1024]{1,0:T(8,128)(2,1)}, u32[]{:S(2)}) copy-start(bf16[512,1024]{1,0:T(8,128)(2,1)} %param.4) | copy-start | bytes 3145732
  26.4 7.3 %collective-permute-start.2 = (bf16[512,1024]{1,0:T(8,128)(2,1)}, bf16[512,1024]{1,0:T(8,128)(2,1)S(1)}, u32[]{:S(2)}, u32[]{:S(2)}) collective-permute-start(bf16[512,1024]{1,0:T(8,128)(2,1)} %collective-permute-done.1), channel_id=1, source_target_pairs={{0,1},{1,0},{2,3},{3,2},{4,5},{5,4},{6,7},{7,6},{8,9},{9,8},{10,11... | collective-permute-start | bytes 3145736 | tf_op jit(solution)/shard_map/ppermute | solution.py:22
  40.6 49.6 %collective-permute-start.8 = (bf16[512,1024]{1,0:T(8,128)(2,1)}, bf16[512,1024]{1,0:T(8,128)(2,1)}, u32[]{:S(2)}, u32[]{:S(2)}) collective-permute-start(bf16[512,1024]{1,0:T(8,128)(2,1)} %shard_map.48), channel_id=1, source_target_pairs={{0,16},{4,20},{8,24},{12,28},{16,0},{20,4},{24,8},{28,12},{1,17},{... | collective-permute-start | bytes 3145736 | tf_op jit(solution)/shard_map/ppermute | solution.py:22
  49.3 47.2 %collective-permute-start.6 = (bf16[512,1024]{1,0:T(8,128)(2,1)}, bf16[512,1024]{1,0:T(8,128)(2,1)}, u32[]{:S(2)}, u32[]{:S(2)}) collective-permute-start(bf16[512,1024]{1,0:T(8,128)(2,1)} %shard_map.47), channel_id=1, source_target_pairs={{0,8},{4,12},{8,0},{12,4},{16,24},{20,28},{24,16},{28,20},{1,9},{5... | collective-permute-start | bytes 3145736 | tf_op jit(solution)/shard_map/ppermute | solution.py:22
  70.8 32.1 %collective-permute-start.4 = (bf16[512,1024]{1,0:T(8,128)(2,1)}, bf16[512,1024]{1,0:T(8,128)(2,1)S(1)}, u32[]{:S(2)}, u32[]{:S(2)}) collective-permute-start(bf16[512,1024]{1,0:T(8,128)(2,1)} %shard_map.46), channel_id=1, source_target_pairs={{0,4},{4,0},{8,12},{12,8},{16,20},{20,16},{24,28},{28,24},{1,5},{5... | collective-permute-start | bytes 3145736 | tf_op jit(solution)/shard_map/ppermute | solution.py:22
  90.2 12.7 %slice-start = ((s8[6291456]{0:T(1024)(128)(4,1)}), s8[4194304]{0:T(1024)(128)(4,1)S(1)}, s32[]{:S(2)}) async-start(s8[6291456]{0:T(1024)(128)(4,1)} %bitcast.13), calls=%async_computation | async-start | bytes 8388608
  96.6 6.3 %slice-start.1 = ((s8[6291456]{0:T(1024)(128)(4,1)}), s8[2097152]{0:T(1024)(128)(4,1)S(1)}, s32[]{:S(2)}) async-start(s8[6291456]{0:T(1024)(128)(4,1)} %bitcast.13), calls=%async_computation.1 | async-start | bytes 4194304

commit v2 on v1

v2 whole, which is shorter than its diff:
```python
import functools

import jax
import jax.numpy as jnp
from jax import lax
from jax.experimental import pallas as pl
from jax.experimental.pallas import tpu as pltpu
from jax.sharding import PartitionSpec as P

H = 32
HD = 32
BLK = 64
KB = 13
N_PARTNER = 3
N_OWN = KB - N_PARTNER
LANES = 256
UNROLL = 2
LOG2E = 1.4426950408889634


def exchange(value, axis, mask):
    pairs = [(source, source ^ mask) for source in range(lax.axis_size(axis))]
    return lax.ppermute(value, axis, pairs)


def gather_shards(value, axis):
    held = {0: value}
    mask = lax.axis_size(axis) // 2
    while mask >= 1:
        for k in list(held):
            held[k ^ mask] = exchange(held[k], axis, mask)
        mask //= 2
    return [held[k] for k in range(len(held))]


def pick_body(index_ref, *refs):
    shard_refs = refs[:-2]
    out_ref, sems = refs[-2:]
    count = out_ref.shape[0] // BLK
    shard_blocks = shard_refs[0].shape[0] // BLK

    def copy_of(i, shard, block):
        return pltpu.make_async_copy(
            shard_refs[shard].at[pl.ds(block * BLK, BLK), :],
            out_ref.at[pl.ds(i * BLK, BLK), :],
            sems.at[i],
        )

    for i in range(count):
        place = index_ref[i]
        for shard in range(len(shard_refs)):

            @pl.when(place // shard_blocks == shard)
            def _():
                copy_of(i, shard, place % shard_blocks).start()

    for i in range(count):
        copy_of(i, 0, 0).wait()


def pick_blocks(shards, index):
    count = index.shape[0]
    width = shards[0].shape[1]
    anywhere = pl.BlockSpec(memory_space=pl.ANY)
    return pl.pallas_call(
        pick_body,
        grid_spec=pltpu.PrefetchScalarGridSpec(
            num_scalar_prefetch=1,
            grid=(1,),
            in_specs=[anywhere] * len(shards),
            out_specs=anywhere,
            scratch_shapes=[pltpu.SemaphoreType.DMA((count,))],
        ),
        out_shape=jax.ShapeDtypeStruct((count * BLK, width), shards[0].dtype),
        cost_estimate=pl.CostEstimate(
            flops=0, bytes_accessed=4 * count * BLK * width, transcendentals=0
        ),
    )(index, *shards)


GROUP_HEADS = LANES // HD
STAT = 128
FACTOR = HD ** (-0.5) * LOG2E


def raw_scores(q, keys):
    head = lax.broadcasted_iota(jnp.int32, (BLK, LANES), 1) // HD
    zero = jnp.zeros_like(q)
    spread = jnp.concatenate(
        [jnp.where(head == h, q, zero) for h in range(GROUP_HEADS)], axis=0
    )
    return lax.dot_general(
        spread, keys, (((1,), (1,)), ((), ())), preferred_element_type=jnp.float32
    )


def fold(values, lane_head):
    shape = lane_head.shape
    out = jnp.broadcast_to(values[0:BLK], shape)
    for h in range(1, GROUP_HEADS):
        out = jnp.where(lane_head == h, values[h * BLK : (h + 1) * BLK], out)
    return out


def own_body(unroll, shard_count, index_ref, q_ref, *refs):
    shard_refs = refs[: 2 * shard_count]
    part_ref, stat_ref, k_all, v_all, k_buf, v_buf = refs[2 * shard_count :]
    step = pl.program_id(1)
    shard_rows = shard_refs[0].shape[0]

    @pl.when(step == 0)
    def _():
        for s in range(shard_count):
            here = slice(s * shard_rows, (s + 1) * shard_rows)
            k_all[here, :] = shard_refs[s][...]
            v_all[here, :] = shard_refs[shard_count + s][...]

    head = lax.broadcasted_iota(jnp.int32, (BLK, LANES), 1) // HD
    stat_lane = lax.broadcasted_iota(jnp.int32, (BLK, STAT), 1)
    for u in range(unroll):
        block = step * unroll + u
        for c in range(N_OWN):
            start = pl.multiple_of(index_ref[block * N_OWN + c] * BLK, BLK)
            k_buf[u, c * BLK : (c + 1) * BLK, :] = k_all[pl.ds(start, BLK), :]
            v_buf[u, c * BLK : (c + 1) * BLK, :] = v_all[pl.ds(start, BLK), :]
        rows = slice(u * BLK, (u + 1) * BLK)
        raw = raw_scores(q_ref[rows, :], k_buf[u])
        top = jnp.max(raw, axis=1, keepdims=True) * FACTOR
        exps = jnp.exp2(raw * FACTOR - top)
        total = jnp.sum(exps, axis=1, keepdims=True)
        result = jnp.dot(
            exps.astype(jnp.bfloat16), v_buf[u], preferred_element_type=jnp.float32
        )
        part_ref[rows, :] = fold(result, head)
        stat_ref[rows, :] = jnp.where(
            stat_lane < GROUP_HEADS,
            fold(top, stat_lane),
            fold(total, stat_lane - GROUP_HEADS),
        )


def attend_own(index, query, own, unroll):
    rows, width = query.shape
    lane_groups = width // LANES
    blocks = rows // BLK
    shard_rows = own[0].shape[0]
    own_rows = shard_rows * len(own)
    here = lambda hg, i, index: (i, hg)
    keys = N_OWN * BLK
    return pl.pallas_call(
        functools.partial(own_body, unroll, len(own)),
        grid_spec=pltpu.PrefetchScalarGridSpec(
            num_scalar_prefetch=1,
            grid=(lane_groups, blocks // unroll),
            in_specs=[pl.BlockSpec((unroll * BLK, LANES), here)]
            + [pl.BlockSpec((shard_rows, LANES), lambda hg, i, index: (0, hg))] * len(own)
            + [pl.BlockSpec((shard_rows, LANES), lambda hg, i, index: (0, lane_groups + hg))]
            * len(own),
            out_specs=[
                pl.BlockSpec((unroll * BLK, LANES), here),
                pl.BlockSpec((unroll * BLK, STAT), here),
            ],
            scratch_shapes=[pltpu.VMEM((own_rows, LANES), jnp.bfloat16)] * 2
            + [pltpu.VMEM((unroll, keys, LANES), jnp.bfloat16)] * 2,
        ),
        out_shape=[
            jax.ShapeDtypeStruct((rows, width), jnp.float32),
            jax.ShapeDtypeStruct((rows, lane_groups * STAT), jnp.float32),
        ],
        compiler_params=pltpu.CompilerParams(vmem_limit_bytes=48 * 1024 * 1024),
        cost_estimate=pl.CostEstimate(
            flops=4 * rows * keys * width * GROUP_HEADS,
            bytes_accessed=own_rows * width * 4,
            transcendentals=rows * keys * H,
        ),
    )(index, query, *own, *own)


def cross_body(unroll, q_ref, part_ref, stat_ref, *refs):
    k_refs = refs[:N_PARTNER]
    v_refs = refs[N_PARTNER : 2 * N_PARTNER]
    out_ref = refs[2 * N_PARTNER]
    head = lax.broadcasted_iota(jnp.int32, (BLK, LANES), 1) // HD
    for u in range(unroll):
        rows = slice(u * BLK, (u + 1) * BLK)
        keys = jnp.concatenate([ref[rows, :] for ref in k_refs], axis=0)
        values = jnp.concatenate([ref[rows, :] for ref in v_refs], axis=0)
        raw = raw_scores(q_ref[rows, :], keys)
        stat = stat_ref[rows, :]
        own_top = jnp.concatenate(
            [stat[:, h : h + 1] for h in range(GROUP_HEADS)], axis=0
        )
        own_total = jnp.concatenate(
            [stat[:, GROUP_HEADS + h : GROUP_HEADS + h + 1] for h in range(GROUP_HEADS)],
            axis=0,
        )
        top = jnp.maximum(jnp.max(raw, axis=1, keepdims=True) * FACTOR, own_top)
        exps = jnp.exp2(raw * FACTOR - top)
        scale = jnp.exp2(own_top - top)
        total = jnp.sum(exps, axis=1, keepdims=True) + own_total * scale
        result = jnp.dot(
            exps.astype(jnp.bfloat16), values, preferred_element_type=jnp.float32
        )
        joint = fold(result, head) + part_ref[rows, :] * fold(scale, head)
        out_ref[rows, :] = (joint / fold(total, head)).astype(jnp.bfloat16)


def attend_cross(query, part, stat, crosses, unroll):
    rows, width = query.shape
    lane_groups = width // LANES
    blocks = rows // BLK
    here = lambda hg, i: (i, hg)
    keys = N_PARTNER * BLK
    wide = pl.BlockSpec((unroll * BLK, LANES), here)
    return pl.pallas_call(
        functools.partial(cross_body, unroll),
        grid=(lane_groups, blocks // unroll),
        in_specs=[wide, wide, pl.BlockSpec((unroll * BLK, STAT), here)]
        + [wide] * N_PARTNER
        + [pl.BlockSpec((unroll * BLK, LANES), lambda hg, i: (i, lane_groups + hg))]
        * N_PARTNER,
        out_specs=wide,
        out_shape=jax.ShapeDtypeStruct((rows, width), jnp.bfloat16),
        compiler_params=pltpu.CompilerParams(vmem_limit_bytes=48 * 1024 * 1024),
        cost_estimate=pl.CostEstimate(
            flops=4 * rows * keys * width * GROUP_HEADS,
            bytes_accessed=rows * width * 20,
            transcendentals=rows * keys * H,
        ),
    )(query, part, stat, *crosses, *crosses)


def project(rows, weights):
    return jnp.dot(rows, weights, preferred_element_type=jnp.float32).astype(jnp.bfloat16)


def per_device(tokens, w_qkv, w_out, block_table):
    groups = lax.axis_size("grp")
    me = lax.axis_index("grp")
    tok_rows, width = tokens.shape
    blocks = tok_rows // BLK
    seg_blocks = blocks * groups

    table = lax.dynamic_slice_in_dim(block_table, me * blocks, blocks, axis=0) % seg_blocks
    place = ((table // blocks) ^ me) * blocks + table % blocks
    asked = [exchange(table[:, N_OWN + j], "seg", 1 << j) for j in range(N_PARTNER)]

    shards = gather_shards(tokens, "grp")
    arrived = []
    for j in reversed(range(N_PARTNER)):
        want = ((asked[j] // blocks) ^ me) * blocks + asked[j] % blocks
        arrived.append(exchange(pick_blocks(shards, want), "seg", 1 << j))
    arrived = arrived[::-1]

    query = project(tokens, w_qkv[:, :width])
    own = [project(shard, w_qkv[:, width:]) for shard in shards]
    part, stat = attend_own(place[:, :N_OWN].reshape(-1), query, own, UNROLL)
    crosses = [project(rows, w_qkv[:, width:]) for rows in arrived]
    attended = attend_cross(query, part, stat, crosses, UNROLL)
    return project(attended, w_out)


def solution(mesh):
    return jax.shard_map(
        per_device,
        mesh=mesh,
        in_specs=(P(("seg", "grp"), None), P(), P(), P("seg", None)),
        out_specs=P(("seg", "grp"), None),
        check_vma=False,
    )
```

time: 163 us -> 247 us (1.52)
  Pallas kernels: 72.2 us -> 182 us
  waiting for transfers between devices: 31.4 us -> 5.57 us
  matrix products: 34.5 us -> 41.4 us
  local copies, waits for them, and re-layouts: 6.92 us -> 0.18 us
    pallas_call x3, Pallas kernels: 17.5 us -> 101 us  [pick_blocks(): pl.pallas_call(pick_body, grid_spec=pltpu.PrefetchScalarGridSpec(num_scal...]
    pallas_call x1 -> x2, Pallas kernels: 54.6 us -> 80.9 us  [the longest x1 50.6 us: attend_cross(): pl.pallas_call(functools.partial(cross_body, unroll), grid=(lane_groups,...]
    ppermute x9, waiting for transfers between devices: 31.4 us -> 5.57 us  [exchange(): return lax.ppermute(value, axis, pairs)]
    dot_general x6 -> x9, matrix products: 34.5 us -> 41.4 us  [project(): jnp.dot(rows, weights, preferred_element_type=jnp.float32)]
    unnamed x11 -> x8, local copies, waits for them, and re-layouts: 5.68 us -> 0.02 us
  transfers between devices with their start and end apart: 9 -> 9, of which waited for: 2 -> 1; matrix products, arithmetic and copies ran while one was open for 24% -> 15% of each run, Pallas kernels for 7% -> 40%
where the time goes in v2:
time: 247 us; the launch traced here: 246 us
  Pallas kernels  182 us (74%)
  matrix products  41.4 us (17%)
  starting transfers between devices  14.8 us (6%)
  waiting for transfers between devices  5.57 us (2%)
    pallas_call x3, Pallas kernels, pick_blocks(): pl.pallas_call(pick_body, grid_spec=pltpu.PrefetchScalarGridSpec(num_scal...  101 us
    pallas_call x1, Pallas kernels, attend_cross(): pl.pallas_call(functools.partial(cross_body, unroll), grid=(lane_groups,...  50.6 us
    dot_general x9, matrix products, project(): jnp.dot(rows, weights, preferred_element_type=jnp.float32)  41.4 us
    pallas_call x1, Pallas kernels, attend_own(): pl.pallas_call(functools.partial(own_body, unroll, len(own)), grid_spec=p...  30.3 us
    ppermute x9, starting transfers between devices, exchange(): return lax.ppermute(value, axis, pairs)  14.8 us
    ppermute x9, waiting for transfers between devices, exchange(): return lax.ppermute(value, axis, pairs)  5.57 us
  transfers between devices with their start and end apart: 9, of which 1 were waited for; matrix products, arithmetic and copies ran while one was open for 15% of the time, Pallas kernels for 40%

profile of v2, /device:TPU:0, one launch (start us, length us, event | category | flops | bytes accessed | tf_op | source)
XLA Modules:
  0.0 246.3 jit_solution(4556678358937197726)
XLA Ops:
  0.0 2.9 %collective-permute-start.1 = (bf16[512,1024]{1,0:T(8,128)(2,1)}, bf16[512,1024]{1,0:T(8,128)(2,1)}, u32[]{:S(2)}, u32[]{:S(2)}) collective-permute-start(bf16[512,1024]{1,0:T(8,128)(2,1)} %refs_0_.5), channel_id=1, source_target_pairs={{0,2},{1,3},{2,0},{3,1},{4,6},{5,7},{6,4},{7,5},{8,10},{9,11},{10,... | collective-permute-start | bytes 3145736 | tf_op jit(solution)/shard_map/ppermute | solution.py:23
  2.9 0.0 collective-permute-start
  2.9 0.8 negate_select_fusion
  3.7 2.7 %collective-permute-start.7 = (s32[8]{0:T(128)S(1)}, s32[8]{0:T(128)S(1)}, u32[]{:S(2)}, u32[]{:S(2)}) collective-permute-start(s32[8]{0:T(128)S(1)} %get-tuple-element.11), channel_id=1, source_target_pairs={{0,16},{4,20},{8,24},{12,28},{16,0},{20,4},{24,8},{28,12},{1,17},{... | collective-permute-start | bytes 104 | tf_op jit(solution)/shard_map/ppermute | solution.py:23
  6.4 1.6 collective-permute-start.5
  8.0 1.5 collective-permute-start.3
  9.5 6.2 %convolution_convert_fusion.6.refs_0_.refs_4_ = bf16[512,2048]{1,0:T(8,128)(2,1)} fusion(bf16[512,1024]{1,0:T(8,128)(2,1)} %refs_0_.5, bf16[1024,3072]{1,0:T(8,128)(2,1)} %param.5), kind=kOutput, calls=%fused_computation.6 | convolution fusion | flops 2148532224 | bytes 7340032 | tf_op jit(solution)/shard_map/dot_general | solution.py:234
  15.7 0.1 copy.5
  15.8 0.1 reshape.3.index_ref
  15.9 3.3 %fusion.2.q_ref = bf16[512,1024]{1,0:T(8,128)(2,1)S(1)} fusion(bf16[512,1024]{1,0:T(8,128)(2,1)} %refs_0_.5, bf16[1024,3072]{1,0:T(8,128)(2,1)} %param.5), kind=kOutput, calls=%fused_computation.9 | convolution fusion | flops 1074266112 | bytes 4194304 | tf_op jit(solution)/shard_map/dot_general | solution.py:234
  19.2 0.0 collective-permute-done.7
  19.2 0.5 fusion.20.index_ref
  19.7 0.5 fusion.19.index_ref
  20.3 0.6 fusion.18.index_ref
  20.9 5.6 %collective-permute-done.1.refs_2_ = bf16[512,1024]{1,0:T(8,128)(2,1)} collective-permute-done((bf16[512,1024]{1,0:T(8,128)(2,1)}, bf16[512,1024]{1,0:T(8,128)(2,1)}, u32[]{:S(2)}, u32[]{:S(2)}) %collective-permute-start.1) | collective-permute-done | bytes 1048608 | tf_op jit(solution)/shard_map/ppermute | solution.py:23
  26.4 4.9 %convolution_convert_fusion.4.refs_2_.refs_6_ = bf16[512,2048]{1,0:T(8,128)(2,1)} fusion(bf16[512,1024]{1,0:T(8,128)(2,1)} %collective-permute-done.1.refs_2_, bf16[1024,3072]{1,0:T(8,128)(2,1)S(1)} %copy-done.1), kind=kOutput, calls=%fused_computation.4 | convolution fusion | flops 2148532224 | bytes 7340032 | tf_op jit(solution)/shard_map/dot_general | solution.py:234
  31.3 0.0 collective-permute-done.refs_1_
  31.3 4.9 %convolution_convert_fusion.5.refs_1_.refs_5_ = bf16[512,2048]{1,0:T(8,128)(2,1)} fusion(bf16[512,1024]{1,0:T(8,128)(2,1)} %collective-permute-done.refs_1_, bf16[1024,3072]{1,0:T(8,128)(2,1)S(1)} %copy-done.1), kind=kOutput, calls=%fused_computation.5 | convolution fusion | flops 2148532224 | bytes 7340032 | tf_op jit(solution)/shard_map/dot_general | solution.py:234
  36.2 0.0 collective-permute-done.2.refs_3_
  36.2 33.6 %shard_map.49 = bf16[512,1024]{1,0:T(8,128)(2,1)} custom-call(s32[8]{0:T(128)} %fusion.20.index_ref, bf16[512,1024]{1,0:T(8,128)(2,1)} %refs_0_.5, bf16[512,1024]{1,0:T(8,128)(2,1)} %collective-permute-done.refs_1_, bf16[512,1024]{1,0:T(8,128)(2,1)} %collective-permute-done.1.refs_2_, bf16[512,1024]{1,0:T(8,128)(2,1)} %collective-permute-done.2.refs_3_), custom_call_target="tpu_custom_call" | custom-call | bytes 2097152 | tf_op jit(solution)/shard_map/pallas_call | solution.py:65
  69.8 2.9 %collective-permute-start.8 = (bf16[512,1024]{1,0:T(8,128)(2,1)}, bf16[512,1024]{1,0:T(8,128)(2,1)}, u32[]{:S(2)}, u32[]{:S(2)}) collective-permute-start(bf16[512,1024]{1,0:T(8,128)(2,1)} %shard_map.49), channel_id=1, source_target_pairs={{0,16},{4,20},{8,24},{12,28},{16,0},{20,4},{24,8},{28,12},{1,17},{... | collective-permute-start | bytes 3145736 | tf_op jit(solution)/shard_map/ppermute | solution.py:23
  72.8 33.6 %shard_map.48 = bf16[512,1024]{1,0:T(8,128)(2,1)} custom-call(s32[8]{0:T(128)} %fusion.19.index_ref, bf16[512,1024]{1,0:T(8,128)(2,1)} %refs_0_.5, bf16[512,1024]{1,0:T(8,128)(2,1)} %collective-permute-done.refs_1_, bf16[512,1024]{1,0:T(8,128)(2,1)} %collective-permute-done.1.refs_2_, bf16[512,1024]{1,0:T(8,128)(2,1)} %collective-permute-done.2.refs_3_), custom_call_target="tpu_custom_call" | custom-call | bytes 2097152 | tf_op jit(solution)/shard_map/pallas_call | solution.py:65
  106.4 1.6 collective-permute-start.6
  108.0 33.6 %shard_map.47 = bf16[512,1024]{1,0:T(8,128)(2,1)} custom-call(s32[8]{0:T(128)} %fusion.18.index_ref, bf16[512,1024]{1,0:T(8,128)(2,1)} %refs_0_.5, bf16[512,1024]{1,0:T(8,128)(2,1)} %collective-permute-done.refs_1_, bf16[512,1024]{1,0:T(8,128)(2,1)} %collective-permute-done.1.refs_2_, bf16[512,1024]{1,0:T(8,128)(2,1)} %collective-permute-done.2.refs_3_), custom_call_target="tpu_custom_call" | custom-call | bytes 2097152 | tf_op jit(solution)/shard_map/pallas_call | solution.py:65
  141.6 1.6 collective-permute-start.4
  143.2 6.4 %convolution_convert_fusion.3.refs_3_.refs_7_ = bf16[512,2048]{1,0:T(8,128)(2,1)} fusion(bf16[512,1024]{1,0:T(8,128)(2,1)} %collective-permute-done.2.refs_3_, bf16[1024,3072]{1,0:T(8,128)(2,1)} %param.5), kind=kOutput, calls=%fused_computation.3 | convolution fusion | flops 2148532224 | bytes 7340032 | tf_op jit(solution)/shard_map/dot_general | solution.py:234
  149.6 30.3 %shard_map.46 = (f32[512,1024]{1,0:T(8,128)S(1)}, f32[512,512]{1,0:T(8,128)S(1)}) custom-call(s32[80]{0:T(128)S(1)} %reshape.3.index_ref, bf16[512,1024]{1,0:T(8,128)(2,1)S(1)} %fusion.2.q_ref, bf16[512,2048]{1,0:T(8,128)(2,1)} %convolution_convert_fusion.6.refs_0_.refs_4_, bf16[512,2048]{1,0:T(8,128)(2,1)} %convolution_convert_fusion.5.refs_1_.refs_5_, ...), custom_call_target="tpu_custom_call" | custom-call | flops 10737418240 | bytes 8388608 | tf_op jit(solution)/shard_map/pallas_call | solution.py:150
  179.9 4.9 %convolution_convert_fusion.refs_2_.refs_5_ = bf16[512,2048]{1,0:T(8,128)(2,1)} fusion(bf16[512,1024]{1,0:T(8,128)(2,1)} %collective-permute-done.8, bf16[1024,3072]{1,0:T(8,128)(2,1)S(1)} %bitcast.17), kind=kOutput, calls=%fused_computation | convolution fusion | flops 2148532224 | bytes 7340032 | tf_op jit(solution)/shard_map/dot_general | solution.py:234
  184.8 4.9 %convolution_convert_fusion.1.refs_1_.refs_4_ = bf16[512,2048]{1,0:T(8,128)(2,1)} fusion(bf16[512,1024]{1,0:T(8,128)(2,1)} %collective-permute-done.6, bf16[1024,3072]{1,0:T(8,128)(2,1)S(1)} %bitcast.17), kind=kOutput, calls=%fused_computation.1 | convolution fusion | flops 2148532224 | bytes 7340032 | tf_op jit(solution)/shard_map/dot_general | solution.py:234
  189.7 3.7 %convolution_convert_fusion.2.refs_0_.refs_3_ = bf16[512,2048]{1,0:T(8,128)(2,1)} fusion(bf16[512,1024]{1,0:T(8,128)(2,1)S(1)} %collective-permute-done.4, bf16[1024,3072]{1,0:T(8,128)(2,1)S(1)} %bitcast.17), kind=kOutput, calls=%fused_computation.2 | convolution fusion | flops 2148532224 | bytes 7340032 | tf_op jit(solution)/shard_map/dot_general | solution.py:234
  193.4 50.6 %shard_map.50 = bf16[512,1024]{1,0:T(8,128)(2,1)S(1)} custom-call(bf16[512,1024]{1,0:T(8,128)(2,1)S(1)} %fusion.2.q_ref, f32[512,1024]{1,0:T(8,128)S(1)} %get-tuple-element.7.part_ref, f32[512,512]{1,0:T(8,128)S(1)} %get-tuple-element.8.stat_ref, bf16[512,2048]{1,0:T(8,128)(2,1)} %convolution_convert_fusion.2.refs_0_.refs_3_, ...), custom_call_target="tpu_custom_call" | custom-call | flops 3221225472 | bytes 10485760 | tf_op jit(solution)/shard_map/pallas_call | solution.py:215
  244.0 2.2 convolution_convert_fusion.7
  (19 shorter events, 0.1 us)
Async XLA Ops:
  0.0 244.0 %copy-start = (bf16[1024,1024]{1,0:T(8,128)(2,1)S(1)}, bf16[1024,1024]{1,0:T(8,128)(2,1)}, u32[]{:S(2)}) copy-start(bf16[1024,1024]{1,0:T(8,128)(2,1)} %param.6) | copy-start | bytes 6291460
  0.0 26.4 %collective-permute-start.1 = (bf16[512,1024]{1,0:T(8,128)(2,1)}, bf16[512,1024]{1,0:T(8,128)(2,1)}, u32[]{:S(2)}, u32[]{:S(2)}) collective-permute-start(bf16[512,1024]{1,0:T(8,128)(2,1)} %refs_0_.5), channel_id=1, source_target_pairs={{0,2},{1,3},{2,0},{3,1},{4,6},{5,7},{6,4},{7,5},{8,10},{9,11},{10,... | collective-permute-start | bytes 3145736 | tf_op jit(solution)/shard_map/ppermute | solution.py:23
  2.9 28.4 %collective-permute-start = (bf16[512,1024]{1,0:T(8,128)(2,1)}, bf16[512,1024]{1,0:T(8,128)(2,1)}, u32[]{:S(2)}, u32[]{:S(2)}) collective-permute-start(bf16[512,1024]{1,0:T(8,128)(2,1)} %refs_0_.5), channel_id=1, source_target_pairs={{0,1},{1,0},{2,3},{3,2},{4,5},{5,4},{6,7},{7,6},{8,9},{9,8},{10,11... | collective-permute-start | bytes 3145736 | tf_op jit(solution)/shard_map/ppermute | solution.py:23
  3.7 15.5 %collective-permute-start.7 = (s32[8]{0:T(128)S(1)}, s32[8]{0:T(128)S(1)}, u32[]{:S(2)}, u32[]{:S(2)}) collective-permute-start(s32[8]{0:T(128)S(1)} %get-tuple-element.11), channel_id=1, source_target_pairs={{0,16},{4,20},{8,24},{12,28},{16,0},{20,4},{24,8},{28,12},{1,17},{... | collective-permute-start | bytes 104 | tf_op jit(solution)/shard_map/ppermute | solution.py:23
  6.4 13.3 %collective-permute-start.5 = (s32[8]{0:T(128)S(1)}, s32[8]{0:T(128)S(1)}, u32[]{:S(2)}, u32[]{:S(2)}) collective-permute-start(s32[8]{0:T(128)S(1)} %get-tuple-element.12), channel_id=1, source_target_pairs={{0,8},{4,12},{8,0},{12,4},{16,24},{20,28},{24,16},{28,20},{1,9},{5... | collective-permute-start | bytes 104 | tf_op jit(solution)/shard_map/ppermute | solution.py:23
  8.0 12.3 %collective-permute-start.3 = (s32[8]{0:T(128)S(1)}, s32[8]{0:T(128)S(1)}, u32[]{:S(2)}, u32[]{:S(2)}) collective-permute-start(s32[8]{0:T(128)S(1)} %get-tuple-element.13), channel_id=1, source_target_pairs={{0,4},{4,0},{8,12},{12,8},{16,20},{20,16},{24,28},{28,24},{1,5},{5... | collective-permute-start | bytes 104 | tf_op jit(solution)/shard_map/ppermute | solution.py:23
  15.9 10.5 %copy-start.1 = (bf16[1024,3072]{1,0:T(8,128)(2,1)S(1)}, bf16[1024,3072]{1,0:T(8,128)(2,1)}, u32[]{:S(2)}) copy-start(bf16[1024,3072]{1,0:T(8,128)(2,1)} %param.5) | copy-start | bytes 18874372
  26.4 9.8 %collective-permute-start.2 = (bf16[512,1024]{1,0:T(8,128)(2,1)}, bf16[512,1024]{1,0:T(8,128)(2,1)}, u32[]{:S(2)}, u32[]{:S(2)}) collective-permute-start(bf16[512,1024]{1,0:T(8,128)(2,1)} %collective-permute-done.1.refs_2_), channel_id=1, source_target_pairs={{0,1},{1,0},{2,3},{3,2},{4,5},{5,4},{6,7},{7,6},{8,9},{9,8},{10,11... | collective-permute-start | bytes 3145736 | tf_op jit(solution)/shard_map/ppermute | solution.py:23
  69.8 110.0 %collective-permute-start.8 = (bf16[512,1024]{1,0:T(8,128)(2,1)}, bf16[512,1024]{1,0:T(8,128)(2,1)}, u32[]{:S(2)}, u32[]{:S(2)}) collective-permute-start(bf16[512,1024]{1,0:T(8,128)(2,1)} %shard_map.49), channel_id=1, source_target_pairs={{0,16},{4,20},{8,24},{12,28},{16,0},{20,4},{24,8},{28,12},{1,17},{... | collective-permute-start | bytes 3145736 | tf_op jit(solution)/shard_map/ppermute | solution.py:23
  106.4 78.5 %collective-permute-start.6 = (bf16[512,1024]{1,0:T(8,128)(2,1)}, bf16[512,1024]{1,0:T(8,128)(2,1)}, u32[]{:S(2)}, u32[]{:S(2)}) collective-permute-start(bf16[512,1024]{1,0:T(8,128)(2,1)} %shard_map.48), channel_id=1, source_target_pairs={{0,8},{4,12},{8,0},{12,4},{16,24},{20,28},{24,16},{28,20},{1,9},{5... | collective-permute-start | bytes 3145736 | tf_op jit(solution)/shard_map/ppermute | solution.py:23
  141.6 48.1 %collective-permute-start.4 = (bf16[512,1024]{1,0:T(8,128)(2,1)}, bf16[512,1024]{1,0:T(8,128)(2,1)S(1)}, u32[]{:S(2)}, u32[]{:S(2)}) collective-permute-start(bf16[512,1024]{1,0:T(8,128)(2,1)} %shard_map.47), channel_id=1, source_target_pairs={{0,4},{4,0},{8,12},{12,8},{16,20},{20,16},{24,28},{28,24},{1,5},{5... | collective-permute-start | bytes 3145736 | tf_op jit(solution)/shard_map/ppermute | solution.py:23
  143.2 36.7 %slice-start = ((s8[6291456]{0:T(1024)(128)(4,1)}), s8[4194304]{0:T(1024)(128)(4,1)S(1)}, s32[]{:S(2)}) async-start(s8[6291456]{0:T(1024)(128)(4,1)} %bitcast.16), calls=%async_computation | async-start | bytes 8388608
  149.6 30.3 %slice-start.1 = ((s8[6291456]{0:T(1024)(128)(4,1)}), s8[2097152]{0:T(1024)(128)(4,1)S(1)}, s32[]{:S(2)}) async-start(s8[6291456]{0:T(1024)(128)(4,1)} %bitcast.16), calls=%async_computation.1 | async-start | bytes 4194304

commit v3 on v1

v3 whole, which is shorter than its diff:
```python
import functools

import jax
import jax.numpy as jnp
from jax import lax
from jax.experimental import pallas as pl
from jax.experimental.pallas import tpu as pltpu
from jax.sharding import PartitionSpec as P

H = 32
HD = 32
BLK = 64
KB = 13
N_PARTNER = 3
N_OWN = KB - N_PARTNER
LANES = 256
UNROLL = 2
PARTS = 2
LOG2E = 1.4426950408889634


def exchange(value, axis, mask):
    pairs = [(source, source ^ mask) for source in range(lax.axis_size(axis))]
    return lax.ppermute(value, axis, pairs)


def gather_shards(value, axis):
    held = {0: value}
    mask = lax.axis_size(axis) // 2
    while mask >= 1:
        for k in list(held):
            held[k ^ mask] = exchange(held[k], axis, mask)
        mask //= 2
    return [held[k] for k in range(len(held))]


def pick_body(index_ref, *refs):
    shard_refs = refs[: -N_PARTNER - 1]
    out_refs = refs[-N_PARTNER - 1 : -1]
    sems = refs[-1]
    count = out_refs[0].shape[0] // BLK
    shard_blocks = shard_refs[0].shape[0] // BLK

    def copy_of(j, i, shard, block):
        return pltpu.make_async_copy(
            shard_refs[shard].at[pl.ds(pl.multiple_of(block * BLK, BLK), BLK), :],
            out_refs[j].at[pl.ds(i * BLK, BLK), :],
            sems.at[j * count + i],
        )

    for j in range(N_PARTNER):
        for i in range(count):
            place = index_ref[j * count + i]
            for shard in range(len(shard_refs)):

                @pl.when(place // shard_blocks == shard)
                def _():
                    copy_of(j, i, shard, place % shard_blocks).start()

    for j in range(N_PARTNER):
        for i in range(count):
            copy_of(j, i, 0, 0).wait()


def pick_blocks(shards, index):
    count = index.shape[0] // N_PARTNER
    width = shards[0].shape[1]
    return pl.pallas_call(
        pick_body,
        grid_spec=pltpu.PrefetchScalarGridSpec(
            num_scalar_prefetch=1,
            grid=(1,),
            in_specs=[pl.BlockSpec(memory_space=pl.ANY)] * len(shards),
            out_specs=[pl.BlockSpec((count * BLK, width), lambda i, index: (0, 0))] * N_PARTNER,
            scratch_shapes=[pltpu.SemaphoreType.DMA((N_PARTNER * count,))],
        ),
        out_shape=[jax.ShapeDtypeStruct((count * BLK, width), shards[0].dtype)] * N_PARTNER,
        compiler_params=pltpu.CompilerParams(vmem_limit_bytes=32 * 1024 * 1024),
        cost_estimate=pl.CostEstimate(
            flops=0, bytes_accessed=4 * N_PARTNER * count * BLK * width, transcendentals=0
        ),
    )(index, *shards)


GROUP_HEADS = LANES // HD
FACTOR = HD ** (-0.5) * LOG2E


def attend_body(unroll, shard_count, index_ref, q_ref, *refs):
    shard_refs = refs[: 2 * shard_count]
    refs = refs[2 * shard_count :]
    kc_refs = refs[:N_PARTNER]
    vc_refs = refs[N_PARTNER : 2 * N_PARTNER]
    out_ref, k_all, v_all, k_buf, v_buf = refs[2 * N_PARTNER :]
    step = pl.program_id(1)
    shard_rows = shard_refs[0].shape[0]

    @pl.when(step == 0)
    def _():
        for s in range(shard_count):
            here = slice(s * shard_rows, (s + 1) * shard_rows)
            k_all[here, :] = shard_refs[s][...]
            v_all[here, :] = shard_refs[shard_count + s][...]

    head = lax.broadcasted_iota(jnp.int32, (BLK, LANES), 1) // HD
    for u in range(unroll):
        rows = slice(u * BLK, (u + 1) * BLK)
        for c in range(KB):
            here = slice(c * BLK, (c + 1) * BLK)
            if c < N_OWN:
                place = index_ref[(step * unroll + u) * N_OWN + c]
                there = pl.ds(pl.multiple_of(place * BLK, BLK), BLK)
                k_buf[u, here, :] = k_all[there, :]
                v_buf[u, here, :] = v_all[there, :]
            else:
                k_buf[u, here, :] = kc_refs[c - N_OWN][rows, :]
                v_buf[u, here, :] = vc_refs[c - N_OWN][rows, :]
    for u in range(unroll):
        rows = slice(u * BLK, (u + 1) * BLK)
        q = q_ref[rows, :]
        zero = jnp.zeros_like(q)
        spread = jnp.concatenate(
            [jnp.where(head == h, q, zero) for h in range(GROUP_HEADS)], axis=0
        )
        raw = lax.dot_general(
            spread, k_buf[u], (((1,), (1,)), ((), ())), preferred_element_type=jnp.float32
        )
        top = jnp.max(raw, axis=1, keepdims=True) * FACTOR
        exps = jnp.exp2(raw * FACTOR - top)
        total = jnp.sum(exps, axis=1, keepdims=True)
        result = jnp.dot(
            exps.astype(jnp.bfloat16), v_buf[u], preferred_element_type=jnp.float32
        )
        result = result / total
        out = result[0:BLK]
        for h in range(1, GROUP_HEADS):
            out = jnp.where(head == h, result[h * BLK : (h + 1) * BLK], out)
        out_ref[rows, :] = out.astype(jnp.bfloat16)


def attend(index, query, first, own, crosses):
    rows = crosses[0].shape[0]
    width = query.shape[1]
    lane_groups = width // LANES
    blocks = rows // BLK
    unroll = min(UNROLL, blocks)
    shard_rows = own[0].shape[0]
    own_rows = shard_rows * len(own)
    here = lambda hg, i, index: (i, hg)
    value_here = lambda hg, i, index: (i, lane_groups + hg)
    skip = first // unroll
    keys = KB * BLK
    part = (unroll * BLK, LANES)
    return pl.pallas_call(
        functools.partial(attend_body, unroll, len(own)),
        grid_spec=pltpu.PrefetchScalarGridSpec(
            num_scalar_prefetch=1,
            grid=(lane_groups, blocks // unroll),
            in_specs=[pl.BlockSpec(part, lambda hg, i, index: (skip + i, hg))]
            + [pl.BlockSpec((shard_rows, LANES), lambda hg, i, index: (0, hg))] * len(own)
            + [pl.BlockSpec((shard_rows, LANES), lambda hg, i, index: (0, lane_groups + hg))]
            * len(own)
            + [pl.BlockSpec(part, here)] * N_PARTNER
            + [pl.BlockSpec(part, value_here)] * N_PARTNER,
            out_specs=pl.BlockSpec(part, here),
            scratch_shapes=[pltpu.VMEM((own_rows, LANES), jnp.bfloat16)] * 2
            + [pltpu.VMEM((unroll, keys, LANES), jnp.bfloat16)] * 2,
        ),
        out_shape=jax.ShapeDtypeStruct((rows, width), jnp.bfloat16),
        compiler_params=pltpu.CompilerParams(vmem_limit_bytes=48 * 1024 * 1024),
        cost_estimate=pl.CostEstimate(
            flops=4 * rows * keys * width * GROUP_HEADS,
            bytes_accessed=own_rows * width * 4,
            transcendentals=rows * keys * H,
        ),
    )(index, query, *own, *own, *crosses, *crosses)


def project(rows, weights):
    return jnp.dot(rows, weights, preferred_element_type=jnp.float32).astype(jnp.bfloat16)


def per_device(tokens, w_qkv, w_out, block_table):
    groups = lax.axis_size("grp")
    me = lax.axis_index("grp")
    tok_rows, width = tokens.shape
    blocks = tok_rows // BLK
    seg_blocks = blocks * groups

    table = lax.dynamic_slice_in_dim(block_table, me * blocks, blocks, axis=0) % seg_blocks
    place = ((table // blocks) ^ me) * blocks + table % blocks
    asked = [exchange(table[:, N_OWN + j], "seg", 1 << j) for j in range(N_PARTNER)]

    shards = gather_shards(tokens, "grp")
    want = [((a // blocks) ^ me) * blocks + a % blocks for a in asked]
    size = blocks // PARTS
    picked = []
    for part in range(PARTS):
        here = slice(part * size, (part + 1) * size)
        picked.append(pick_blocks(shards, jnp.concatenate([w[here] for w in want])))
    arrived = [
        [exchange(rows, "seg", 1 << j) for j, rows in enumerate(parts)] for parts in picked
    ]

    w_q, w_kv = w_qkv[:, :width], w_qkv[:, width:]
    query = project(tokens, w_q)
    own = [project(shard, w_kv) for shard in shards]
    mixed = []
    for part in range(PARTS):
        first = part * size
        index = place[first : first + size, :N_OWN].reshape(-1)
        crosses = [project(rows, w_kv) for rows in arrived[part]]
        mixed.append(project(attend(index, query, first, own, crosses), w_out))
    return jnp.concatenate(mixed, axis=0)


def solution(mesh):
    return jax.shard_map(
        per_device,
        mesh=mesh,
        in_specs=(P(("seg", "grp"), None), P(), P(), P("seg", None)),
        out_specs=P(("seg", "grp"), None),
        check_vma=False,
    )
```

time: 163 us -> 144 us (0.88)
  Pallas kernels: 72.2 us -> 47.2 us
  waiting for transfers between devices: 31.4 us -> 40.8 us
  local copies, waits for them, and re-layouts: 6.92 us -> 0.67 us
  starting transfers between devices: 14.6 us -> 18.7 us
    pallas_call x1 -> x2, Pallas kernels: 54.6 us -> 41.7 us  [attend(): pl.pallas_call(functools.partial(attend_body, unroll, len(own)), grid_spe...]
    pallas_call x3 -> x2, Pallas kernels: 17.5 us -> 5.44 us  [pick_blocks(): pl.pallas_call(pick_body, grid_spec=pltpu.PrefetchScalarGridSpec(num_scal...]
    ppermute x9 -> x12, waiting for transfers between devices: 31.4 us -> 40.8 us  [exchange(): return lax.ppermute(value, axis, pairs)]
    unnamed x11 -> x12, local copies, waits for them, and re-layouts: 5.68 us -> 0.03 us
    ppermute x9 -> x12, starting transfers between devices: 14.6 us -> 18.7 us  [exchange(): return lax.ppermute(value, axis, pairs)]
    dot_general x6 -> x13, matrix products: 34.5 us -> 34.2 us  [project(): jnp.dot(rows, weights, preferred_element_type=jnp.float32)]
  transfers between devices with their start and end apart: 9 -> 12, of which waited for: 2 -> 4; matrix products, arithmetic and copies ran while one was open for 24% -> 24% of each run, Pallas kernels for 7% -> 16%
where the time goes in v3:
time: 144 us
  Pallas kernels  47.2 us (33%)
  waiting for transfers between devices  40.8 us (28%)
  matrix products  34.2 us (24%)
  starting transfers between devices  18.7 us (13%)
  other arithmetic  2.01 us (1%)
    pallas_call x2, Pallas kernels, attend(): pl.pallas_call(functools.partial(attend_body, unroll, len(own)), grid_spe...  41.7 us
    ppermute x12, waiting for transfers between devices, exchange(): return lax.ppermute(value, axis, pairs)  40.8 us
    dot_general x13, matrix products, project(): jnp.dot(rows, weights, preferred_element_type=jnp.float32)  34.2 us
    ppermute x12, starting transfers between devices, exchange(): return lax.ppermute(value, axis, pairs)  18.7 us
    pallas_call x2, Pallas kernels, pick_blocks(): pl.pallas_call(pick_body, grid_spec=pltpu.PrefetchScalarGridSpec(num_scal...  5.44 us
  transfers between devices with their start and end apart: 12, of which 4 were waited for; matrix products, arithmetic and copies ran while one was open for 24% of the time, Pallas kernels for 16%

profile of v3, /device:TPU:0, one launch (start us, length us, event | category | flops | bytes accessed | tf_op | source)
XLA Modules:
  0.0 143.8 jit_solution(16979529705429250027)
XLA Ops:
  0.0 2.9 %collective-permute-start.1 = (bf16[512,1024]{1,0:T(8,128)(2,1)}, bf16[512,1024]{1,0:T(8,128)(2,1)}, u32[]{:S(2)}, u32[]{:S(2)}) collective-permute-start(bf16[512,1024]{1,0:T(8,128)(2,1)} %refs_0_.3), channel_id=1, source_target_pairs={{0,2},{1,3},{2,0},{3,1},{4,6},{5,7},{6,4},{7,5},{8,10},{9,11},{10,... | collective-permute-start | bytes 3145736 | tf_op jit(solution)/shard_map/ppermute | solution.py:24
  2.9 0.8 fusion.8
  3.7 1.6 %collective-permute-start.3 = (s32[8]{0:T(128)S(1)}, s32[8]{0:T(128)S(1)}, u32[]{:S(2)}, u32[]{:S(2)}) collective-permute-start(s32[8]{0:T(128)S(1)} %get-tuple-element.21), channel_id=1, source_target_pairs={{0,4},{4,0},{8,12},{12,8},{16,20},{20,16},{24,28},{28,24},{1,5},{5... | collective-permute-start | bytes 104 | tf_op jit(solution)/shard_map/ppermute | solution.py:24
  5.3 2.6 %collective-permute-start.5 = (s32[8]{0:T(128)S(1)}, s32[8]{0:T(128)S(1)}, u32[]{:S(2)}, u32[]{:S(2)}) collective-permute-start(s32[8]{0:T(128)S(1)} %get-tuple-element.22), channel_id=1, source_target_pairs={{0,16},{4,20},{8,24},{12,28},{16,0},{20,4},{24,8},{28,12},{1,17},{... | collective-permute-start | bytes 104 | tf_op jit(solution)/shard_map/ppermute | solution.py:24
  7.9 1.6 %collective-permute-start.4 = (s32[8]{0:T(128)S(1)}, s32[8]{0:T(128)S(1)}, u32[]{:S(2)}, u32[]{:S(2)}) collective-permute-start(s32[8]{0:T(128)S(1)} %get-tuple-element.23), channel_id=1, source_target_pairs={{0,8},{4,12},{8,0},{12,4},{16,24},{20,28},{24,16},{28,20},{1,9},{5... | collective-permute-start | bytes 104 | tf_op jit(solution)/shard_map/ppermute | solution.py:24
  9.5 4.7 %fusion.2.q_ref = bf16[512,1024]{1,0:T(8,128)(2,1)} fusion(bf16[512,1024]{1,0:T(8,128)(2,1)} %refs_0_.3, bf16[1024,3072]{1,0:T(8,128)(2,1)} %param.5), kind=kOutput, calls=%fused_computation.12 | convolution fusion | flops 1074266112 | bytes 4194304 | tf_op jit(solution)/shard_map/dot_general | solution.py:180
  14.2 3.7 %convolution_convert_fusion.3.refs_0_.refs_4_ = bf16[512,2048]{1,0:T(8,128)(2,1)} fusion(bf16[512,1024]{1,0:T(8,128)(2,1)S(1)} %copy-done.1, bf16[1024,3072]{1,0:T(8,128)(2,1)S(1)} %copy-done.3), kind=kOutput, calls=%fused_computation.3 | convolution fusion | flops 2148532224 | bytes 7340032 | tf_op jit(solution)/shard_map/dot_general | solution.py:180
  18.7 7.7 %collective-permute-done.1.refs_2_ = bf16[512,1024]{1,0:T(8,128)(2,1)} collective-permute-done((bf16[512,1024]{1,0:T(8,128)(2,1)}, bf16[512,1024]{1,0:T(8,128)(2,1)}, u32[]{:S(2)}, u32[]{:S(2)}) %collective-permute-start.1) | collective-permute-done | bytes 1048608 | tf_op jit(solution)/shard_map/ppermute | solution.py:24
  26.4 6.2 %convolution_convert_fusion.1.refs_2_.refs_6_ = bf16[512,2048]{1,0:T(8,128)(2,1)} fusion(bf16[512,1024]{1,0:T(8,128)(2,1)} %collective-permute-done.1.refs_2_, bf16[1024,3072]{1,0:T(8,128)(2,1)} %param.5), kind=kOutput, calls=%fused_computation.1 | convolution fusion | flops 2148532224 | bytes 7340032 | tf_op jit(solution)/shard_map/dot_general | solution.py:180
  32.6 4.9 %convolution_convert_fusion.2.refs_1_.refs_5_ = bf16[512,2048]{1,0:T(8,128)(2,1)} fusion(bf16[512,1024]{1,0:T(8,128)(2,1)} %collective-permute-done.refs_1_, bf16[1024,3072]{1,0:T(8,128)(2,1)S(1)} %bitcast.22), kind=kOutput, calls=%fused_computation.2 | convolution fusion | flops 2148532224 | bytes 7340032 | tf_op jit(solution)/shard_map/dot_general | solution.py:180
  37.5 2.7 %shard_map.48 = (bf16[256,1024]{1,0:T(8,128)(2,1)S(1)}, bf16[256,1024]{1,0:T(8,128)(2,1)S(1)}, bf16[256,1024]{1,0:T(8,128)(2,1)S(1)}) custom-call(s32[12]{0:T(128)S(1)} %pad_add_fusion.1.index_ref, bf16[512,1024]{1,0:T(8,128)(2,1)S(1)} %copy-done.1, bf16[512,1024]{1,0:T(8,128)(2,1)} %collective-permute-done.refs_1_, ...), custom_call_target="tpu_custom_call" | custom-call | bytes 3145728 | tf_op jit(solution)/shard_map/pallas_call | solution.py:68
  40.2 1.7 %collective-permute-start.9 = (bf16[256,1024]{1,0:T(8,128)(2,1)S(1)}, bf16[256,1024]{1,0:T(8,128)(2,1)}, u32[]{:S(2)}, u32[]{:S(2)}) collective-permute-start(bf16[256,1024]{1,0:T(8,128)(2,1)S(1)} %get-tuple-element.14), channel_id=1, source_target_pairs={{0,4},{4,0},{8,12},{12,8},{16,20},{20,16},{24,28},{28,24},{1,5},{5... | collective-permute-start | bytes 1572872 | tf_op jit(solution)/shard_map/ppermute | solution.py:24
  41.9 1.8 %collective-permute-start.10 = (bf16[256,1024]{1,0:T(8,128)(2,1)S(1)}, bf16[256,1024]{1,0:T(8,128)(2,1)}, u32[]{:S(2)}, u32[]{:S(2)}) collective-permute-start(bf16[256,1024]{1,0:T(8,128)(2,1)S(1)} %get-tuple-element.15), channel_id=1, source_target_pairs={{0,8},{4,12},{8,0},{12,4},{16,24},{20,28},{24,16},{28,20},{1,9},{5... | collective-permute-start | bytes 1572872 | tf_op jit(solution)/shard_map/ppermute | solution.py:24
  43.7 2.4 %collective-permute-start.11 = (bf16[256,1024]{1,0:T(8,128)(2,1)S(1)}, bf16[256,1024]{1,0:T(8,128)(2,1)S(1)}, u32[]{:S(2)}, u32[]{:S(2)}) collective-permute-start(bf16[256,1024]{1,0:T(8,128)(2,1)S(1)} %get-tuple-element.16), channel_id=1, source_target_pairs={{0,16},{4,20},{8,24},{12,28},{16,0},{20,4},{24,8},{28,12},{1,17},{... | collective-permute-start | bytes 1572872 | tf_op jit(solution)/shard_map/ppermute | solution.py:24
  46.1 2.7 %shard_map.46 = (bf16[256,1024]{1,0:T(8,128)(2,1)S(1)}, bf16[256,1024]{1,0:T(8,128)(2,1)S(1)}, bf16[256,1024]{1,0:T(8,128)(2,1)S(1)}) custom-call(s32[12]{0:T(128)S(1)} %pad_add_fusion.index_ref, bf16[512,1024]{1,0:T(8,128)(2,1)S(1)} %copy-done.1, bf16[512,1024]{1,0:T(8,128)(2,1)} %collective-permute-done.refs_1_, ...), custom_call_target="tpu_custom_call" | custom-call | bytes 3145728 | tf_op jit(solution)/shard_map/pallas_call | solution.py:68
  48.9 0.9 collective-permute-start.7
  49.9 3.7 %convolution_convert_fusion.refs_3_.refs_7_ = bf16[512,2048]{1,0:T(8,128)(2,1)} fusion(bf16[512,1024]{1,0:T(8,128)(2,1)S(1)} %collective-permute-done.2.refs_3_, bf16[1024,3072]{1,0:T(8,128)(2,1)S(1)} %bitcast.22), kind=kOutput, calls=%fused_computation | convolution fusion | flops 2148532224 | bytes 7340032 | tf_op jit(solution)/shard_map/dot_general | solution.py:180
  53.6 11.9 %collective-permute-done.6 = bf16[256,1024]{1,0:T(8,128)(2,1)S(1)} collective-permute-done((bf16[256,1024]{1,0:T(8,128)(2,1)S(1)}, bf16[256,1024]{1,0:T(8,128)(2,1)S(1)}, u32[]{:S(2)}, u32[]{:S(2)}) %collective-permute-start.6) | collective-permute-done | bytes 524320 | tf_op jit(solution)/shard_map/ppermute | solution.py:24
  65.6 3.2 %collective-permute-start.8 = (bf16[256,1024]{1,0:T(8,128)(2,1)S(1)}, bf16[256,1024]{1,0:T(8,128)(2,1)S(1)}, u32[]{:S(2)}, u32[]{:S(2)}) collective-permute-start(bf16[256,1024]{1,0:T(8,128)(2,1)S(1)} %get-tuple-element.13), channel_id=1, source_target_pairs={{0,16},{4,20},{8,24},{12,28},{16,0},{20,4},{24,8},{28,12},{1,17},{... | collective-permute-start | bytes 1572872 | tf_op jit(solution)/shard_map/ppermute | solution.py:24
  68.7 1.2 convolution_convert_fusion.9.refs_8_.refs_11_
  70.0 19.1 %collective-permute-done.7 = bf16[256,1024]{1,0:T(8,128)(2,1)S(1)} collective-permute-done((bf16[256,1024]{1,0:T(8,128)(2,1)S(1)}, bf16[256,1024]{1,0:T(8,128)(2,1)S(1)}, u32[]{:S(2)}, u32[]{:S(2)}) %collective-permute-start.7) | collective-permute-done | bytes 524320 | tf_op jit(solution)/shard_map/ppermute | solution.py:24
  89.0 1.2 convolution_convert_fusion.8.refs_9_.refs_12_
  90.3 2.1 %collective-permute-done.8 = bf16[256,1024]{1,0:T(8,128)(2,1)S(1)} collective-permute-done((bf16[256,1024]{1,0:T(8,128)(2,1)S(1)}, bf16[256,1024]{1,0:T(8,128)(2,1)S(1)}, u32[]{:S(2)}, u32[]{:S(2)}) %collective-permute-start.8) | collective-permute-done | bytes 524320 | tf_op jit(solution)/shard_map/ppermute | solution.py:24
  92.4 1.3 convolution_convert_fusion.7.refs_10_.refs_13_
  93.7 21.0 %shard_map.47 = bf16[256,1024]{1,0:T(8,128)(2,1)S(1)} custom-call(s32[40]{0:T(128)S(1)} %reshape.6.index_ref, bf16[512,1024]{1,0:T(8,128)(2,1)S(1)} %copy-done.2, bf16[512,2048]{1,0:T(8,128)(2,1)} %convolution_convert_fusion.3.refs_0_.refs_4_, bf16[512,2048]{1,0:T(8,128)(2,1)} %convolution_convert_fusion.2.refs_1_.refs_5_, ...), custom_call_target="tpu_custom_call" | custom-call | flops 6979321856 | bytes 8388608 | tf_op jit(solution)/shard_map/pallas_call | solution.py:154
  114.7 2.3 %convolution_convert_fusion.6.refs_8_.refs_11_ = bf16[256,2048]{1,0:T(8,128)(2,1)S(1)} fusion(bf16[256,1024]{1,0:T(8,128)(2,1)} %collective-permute-done.9, bf16[1024,3072]{1,0:T(8,128)(2,1)S(1)} %bitcast.22), kind=kOutput, calls=%fused_computation.6 | convolution fusion | flops 1074266112 | bytes 5767168 | tf_op jit(solution)/shard_map/dot_general | solution.py:180
  117.0 0.7 convolution_convert_fusion.11
  117.7 2.3 %convolution_convert_fusion.5.refs_9_.refs_12_ = bf16[256,2048]{1,0:T(8,128)(2,1)S(1)} fusion(bf16[256,1024]{1,0:T(8,128)(2,1)} %collective-permute-done.10, bf16[1024,3072]{1,0:T(8,128)(2,1)S(1)} %bitcast.22), kind=kOutput, calls=%fused_computation.5 | convolution fusion | flops 1074266112 | bytes 5767168 | tf_op jit(solution)/shard_map/dot_general | solution.py:180
  120.0 1.3 convolution_convert_fusion.4.refs_10_.refs_13_
  121.3 20.8 %shard_map.49 = bf16[256,1024]{1,0:T(8,128)(2,1)S(1)} custom-call(s32[40]{0:T(128)S(1)} %reshape.7.index_ref, bf16[512,1024]{1,0:T(8,128)(2,1)S(1)} %copy-done.2, bf16[512,2048]{1,0:T(8,128)(2,1)} %convolution_convert_fusion.3.refs_0_.refs_4_, bf16[512,2048]{1,0:T(8,128)(2,1)} %convolution_convert_fusion.2.refs_1_.refs_5_, ...), custom_call_target="tpu_custom_call" | custom-call | flops 6979321856 | bytes 8388608 | tf_op jit(solution)/shard_map/pallas_call | solution.py:154
  142.1 0.7 convolution_convert_fusion.10
  142.8 1.0 pad_maximum_fusion
  (37 shorter events, 0.9 us)
Async XLA Ops:
  0.0 117.0 %copy-start = (bf16[1024,1024]{1,0:T(8,128)(2,1)S(1)}, bf16[1024,1024]{1,0:T(8,128)(2,1)}, u32[]{:S(2)}) copy-start(bf16[1024,1024]{1,0:T(8,128)(2,1)} %param.6) | copy-start | bytes 6291460
  0.0 26.4 %collective-permute-start.1 = (bf16[512,1024]{1,0:T(8,128)(2,1)}, bf16[512,1024]{1,0:T(8,128)(2,1)}, u32[]{:S(2)}, u32[]{:S(2)}) collective-permute-start(bf16[512,1024]{1,0:T(8,128)(2,1)} %refs_0_.3), channel_id=1, source_target_pairs={{0,2},{1,3},{2,0},{3,1},{4,6},{5,7},{6,4},{7,5},{8,10},{9,11},{10,... | collective-permute-start | bytes 3145736 | tf_op jit(solution)/shard_map/ppermute | solution.py:24
  2.9 29.7 %collective-permute-start = (bf16[512,1024]{1,0:T(8,128)(2,1)}, bf16[512,1024]{1,0:T(8,128)(2,1)}, u32[]{:S(2)}, u32[]{:S(2)}) collective-permute-start(bf16[512,1024]{1,0:T(8,128)(2,1)} %refs_0_.3), channel_id=1, source_target_pairs={{0,1},{1,0},{2,3},{3,2},{4,5},{5,4},{6,7},{7,6},{8,9},{9,8},{10,11... | collective-permute-start | bytes 3145736 | tf_op jit(solution)/shard_map/ppermute | solution.py:24
  3.7 14.6 %collective-permute-start.3 = (s32[8]{0:T(128)S(1)}, s32[8]{0:T(128)S(1)}, u32[]{:S(2)}, u32[]{:S(2)}) collective-permute-start(s32[8]{0:T(128)S(1)} %get-tuple-element.21), channel_id=1, source_target_pairs={{0,4},{4,0},{8,12},{12,8},{16,20},{20,16},{24,28},{28,24},{1,5},{5... | collective-permute-start | bytes 104 | tf_op jit(solution)/shard_map/ppermute | solution.py:24
  5.3 13.0 %collective-permute-start.5 = (s32[8]{0:T(128)S(1)}, s32[8]{0:T(128)S(1)}, u32[]{:S(2)}, u32[]{:S(2)}) collective-permute-start(s32[8]{0:T(128)S(1)} %get-tuple-element.22), channel_id=1, source_target_pairs={{0,16},{4,20},{8,24},{12,28},{16,0},{20,4},{24,8},{28,12},{1,17},{... | collective-permute-start | bytes 104 | tf_op jit(solution)/shard_map/ppermute | solution.py:24
  7.9 6.2 %copy-start.1 = (bf16[512,1024]{1,0:T(8,128)(2,1)S(1)}, bf16[512,1024]{1,0:T(8,128)(2,1)}, u32[]{:S(2)}) copy-start(bf16[512,1024]{1,0:T(8,128)(2,1)} %refs_0_.3) | copy-start | bytes 3145732
  7.9 6.2 %copy-start.3 = (bf16[1024,3072]{1,0:T(8,128)(2,1)S(1)}, bf16[1024,3072]{1,0:T(8,128)(2,1)}, u32[]{:S(2)}) copy-start(bf16[1024,3072]{1,0:T(8,128)(2,1)} %param.5) | copy-start | bytes 18874372
  7.9 10.5 %collective-permute-start.4 = (s32[8]{0:T(128)S(1)}, s32[8]{0:T(128)S(1)}, u32[]{:S(2)}, u32[]{:S(2)}) collective-permute-start(s32[8]{0:T(128)S(1)} %get-tuple-element.23), channel_id=1, source_target_pairs={{0,8},{4,12},{8,0},{12,4},{16,24},{20,28},{24,16},{28,20},{1,9},{5... | collective-permute-start | bytes 104 | tf_op jit(solution)/shard_map/ppermute | solution.py:24
  18.6 14.0 %slice-start = ((s8[6291456]{0:T(1024)(128)(4,1)}), s8[4194304]{0:T(1024)(128)(4,1)S(1)}, s32[]{:S(2)}) async-start(s8[6291456]{0:T(1024)(128)(4,1)} %bitcast.21), calls=%async_computation | async-start | bytes 8388608
  18.7 13.9 %slice-start.1 = ((s8[6291456]{0:T(1024)(128)(4,1)}), s8[2097152]{0:T(1024)(128)(4,1)S(1)}, s32[]{:S(2)}) async-start(s8[6291456]{0:T(1024)(128)(4,1)} %bitcast.21), calls=%async_computation.1 | async-start | bytes 4194304
  26.4 11.1 %collective-permute-start.2 = (bf16[512,1024]{1,0:T(8,128)(2,1)}, bf16[512,1024]{1,0:T(8,128)(2,1)S(1)}, u32[]{:S(2)}, u32[]{:S(2)}) collective-permute-start(bf16[512,1024]{1,0:T(8,128)(2,1)} %collective-permute-done.1.refs_2_), channel_id=1, source_target_pairs={{0,1},{1,0},{2,3},{3,2},{4,5},{5,4},{6,7},{7,6},{8,9},{9,8},{10,11... | collective-permute-start | bytes 3145736 | tf_op jit(solution)/shard_map/ppermute | solution.py:24
  40.2 74.4 %collective-permute-start.9 = (bf16[256,1024]{1,0:T(8,128)(2,1)S(1)}, bf16[256,1024]{1,0:T(8,128)(2,1)}, u32[]{:S(2)}, u32[]{:S(2)}) collective-permute-start(bf16[256,1024]{1,0:T(8,128)(2,1)S(1)} %get-tuple-element.14), channel_id=1, source_target_pairs={{0,4},{4,0},{8,12},{12,8},{16,20},{20,16},{24,28},{28,24},{1,5},{5... | collective-permute-start | bytes 1572872 | tf_op jit(solution)/shard_map/ppermute | solution.py:24
  41.9 75.8 %collective-permute-start.10 = (bf16[256,1024]{1,0:T(8,128)(2,1)S(1)}, bf16[256,1024]{1,0:T(8,128)(2,1)}, u32[]{:S(2)}, u32[]{:S(2)}) collective-permute-start(bf16[256,1024]{1,0:T(8,128)(2,1)S(1)} %get-tuple-element.15), channel_id=1, source_target_pairs={{0,8},{4,12},{8,0},{12,4},{16,24},{20,28},{24,16},{28,20},{1,9},{5... | collective-permute-start | bytes 1572872 | tf_op jit(solution)/shard_map/ppermute | solution.py:24
  43.7 76.3 %collective-permute-start.11 = (bf16[256,1024]{1,0:T(8,128)(2,1)S(1)}, bf16[256,1024]{1,0:T(8,128)(2,1)S(1)}, u32[]{:S(2)}, u32[]{:S(2)}) collective-permute-start(bf16[256,1024]{1,0:T(8,128)(2,1)S(1)} %get-tuple-element.16), channel_id=1, source_target_pairs={{0,16},{4,20},{8,24},{12,28},{16,0},{20,4},{24,8},{28,12},{1,17},{... | collective-permute-start | bytes 1572872 | tf_op jit(solution)/shard_map/ppermute | solution.py:24
  48.8 16.7 %collective-permute-start.6 = (bf16[256,1024]{1,0:T(8,128)(2,1)S(1)}, bf16[256,1024]{1,0:T(8,128)(2,1)S(1)}, u32[]{:S(2)}, u32[]{:S(2)}) collective-permute-start(bf16[256,1024]{1,0:T(8,128)(2,1)S(1)} %get-tuple-element.11), channel_id=1, source_target_pairs={{0,4},{4,0},{8,12},{12,8},{16,20},{20,16},{24,28},{28,24},{1,5},{5... | collective-permute-start | bytes 1572872 | tf_op jit(solution)/shard_map/ppermute | solution.py:24
  48.9 40.1 %collective-permute-start.7 = (bf16[256,1024]{1,0:T(8,128)(2,1)S(1)}, bf16[256,1024]{1,0:T(8,128)(2,1)S(1)}, u32[]{:S(2)}, u32[]{:S(2)}) collective-permute-start(bf16[256,1024]{1,0:T(8,128)(2,1)S(1)} %get-tuple-element.12), channel_id=1, source_target_pairs={{0,8},{4,12},{8,0},{12,4},{16,24},{20,28},{24,16},{28,20},{1,9},{5... | collective-permute-start | bytes 1572872 | tf_op jit(solution)/shard_map/ppermute | solution.py:24
  65.6 26.9 %collective-permute-start.8 = (bf16[256,1024]{1,0:T(8,128)(2,1)S(1)}, bf16[256,1024]{1,0:T(8,128)(2,1)S(1)}, u32[]{:S(2)}, u32[]{:S(2)}) collective-permute-start(bf16[256,1024]{1,0:T(8,128)(2,1)S(1)} %get-tuple-element.13), channel_id=1, source_target_pairs={{0,16},{4,20},{8,24},{12,28},{16,0},{20,4},{24,8},{28,12},{1,17},{... | collective-permute-start | bytes 1572872 | tf_op jit(solution)/shard_map/ppermute | solution.py:24
  90.3 3.4 %copy-start.2 = (bf16[512,1024]{1,0:T(8,128)(2,1)S(1)}, bf16[512,1024]{1,0:T(8,128)(2,1)}, u32[]{:S(2)}) copy-start(bf16[512,1024]{1,0:T(8,128)(2,1)} %fusion.2.q_ref) | copy-start | bytes 3145732

commit v4 on v3

--- a/solution.py
+++ b/solution.py
@@ -194,17 +194,21 @@
     shards = gather_shards(tokens, "grp")
     want = [((a // blocks) ^ me) * blocks + a % blocks for a in asked]
     size = blocks // PARTS
-    picked = []
+    w_q, w_kv = w_qkv[:, :width], w_qkv[:, width:]
+    query = project(tokens, w_q)
+    own = [project(tokens, w_kv)]
+    arrived = []
     for part in range(PARTS):
         here = slice(part * size, (part + 1) * size)
-        picked.append(pick_blocks(shards, jnp.concatenate([w[here] for w in want])))
-    arrived = [
-        [exchange(rows, "seg", 1 << j) for j, rows in enumerate(parts)] for parts in picked
-    ]
-
-    w_q, w_kv = w_qkv[:, :width], w_qkv[:, width:]
-    query = project(tokens, w_q)
-    own = [project(shard, w_kv) for shard in shards]
+        index = jnp.concatenate([w[here] for w in want])
+        if part == 1:
+            index, arrived[0] = lax.optimization_barrier((index, arrived[0]))
+        picked = pick_blocks(shards, index)
+        if part == 0:
+            picked, later = lax.optimization_barrier((picked, shards[1:]))
+        arrived.append([exchange(rows, "seg", 1 << j) for j, rows in enumerate(picked)])
+        if part == 0:
+            own += [project(shard, w_kv) for shard in later]
     mixed = []
     for part in range(PARTS):
         first = part * size

time: 144 us -> 131 us (0.910)
  waiting for transfers between devices: 40.8 us -> 31.2 us
  matrix products: 34.2 us -> 29.5 us
    ppermute x12, waiting for transfers between devices: 40.8 us -> 31.2 us  [exchange(): return lax.ppermute(value, axis, pairs)]
    dot_general x13, matrix products: 34.2 us -> 29.5 us  [project(): jnp.dot(rows, weights, preferred_element_type=jnp.float32)]
  transfers between devices with their start and end apart: 12 -> 12, of which waited for: 4 -> 5; matrix products, arithmetic and copies ran while one was open for 24% -> 16% of each run, Pallas kernels for 16% -> 16%
where the time goes in v4:
time: 131 us; the launch traced here: 130 us
  Pallas kernels  47.8 us (36%)
  waiting for transfers between devices  31.2 us (24%)
  matrix products  29.5 us (23%)
  starting transfers between devices  17.6 us (13%)
  other arithmetic  2 us (2%)
  local copies, waits for them, and re-layouts  1.41 us (1%)
    pallas_call x2, Pallas kernels, attend(): pl.pallas_call(functools.partial(attend_body, unroll, len(own)), grid_spe...  41.5 us
    ppermute x12, waiting for transfers between devices, exchange(): return lax.ppermute(value, axis, pairs)  31.2 us
    dot_general x13, matrix products, project(): jnp.dot(rows, weights, preferred_element_type=jnp.float32)  29.5 us
    ppermute x12, starting transfers between devices, exchange(): return lax.ppermute(value, axis, pairs)  17.6 us
    pallas_call x2, Pallas kernels, pick_blocks(): pl.pallas_call(pick_body, grid_spec=pltpu.PrefetchScalarGridSpec(num_scal...  6.33 us
  transfers between devices with their start and end apart: 12, of which 5 were waited for; matrix products, arithmetic and copies ran while one was open for 16% of the time, Pallas kernels for 16%

profile of v4, /device:TPU:0, one launch (start us, length us, event | category | flops | bytes accessed | tf_op | source)
XLA Modules:
  0.0 129.8 jit_solution(8529669166315318106)
XLA Ops:
  0.5 2.6 %collective-permute-start.4 = (bf16[512,1024]{1,0:T(8,128)(2,1)}, bf16[512,1024]{1,0:T(8,128)(2,1)}, u32[]{:S(2)}, u32[]{:S(2)}) collective-permute-start(bf16[512,1024]{1,0:T(8,128)(2,1)} %refs_0_.3), channel_id=1, source_target_pairs={{0,2},{1,3},{2,0},{3,1},{4,6},{5,7},{6,4},{7,5},{8,10},{9,11},{10,... | collective-permute-start | bytes 3145736 | tf_op jit(solution)/shard_map/ppermute | solution.py:24
  3.0 0.8 fusion.8
  3.8 2.7 %collective-permute-start.2 = (s32[8]{0:T(128)S(1)}, s32[8]{0:T(128)S(1)}, u32[]{:S(2)}, u32[]{:S(2)}) collective-permute-start(s32[8]{0:T(128)S(1)} %get-tuple-element.42), channel_id=1, source_target_pairs={{0,16},{4,20},{8,24},{12,28},{16,0},{20,4},{24,8},{28,12},{1,17},{... | collective-permute-start | bytes 104 | tf_op jit(solution)/shard_map/ppermute | solution.py:24
  6.5 1.5 %collective-permute-start = (s32[8]{0:T(128)S(1)}, s32[8]{0:T(128)S(1)}, u32[]{:S(2)}, u32[]{:S(2)}) collective-permute-start(s32[8]{0:T(128)S(1)} %get-tuple-element.41), channel_id=1, source_target_pairs={{0,4},{4,0},{8,12},{12,8},{16,20},{20,16},{24,28},{28,24},{1,5},{5... | collective-permute-start | bytes 104 | tf_op jit(solution)/shard_map/ppermute | solution.py:24
  8.0 1.6 %collective-permute-start.1 = (s32[8]{0:T(128)S(1)}, s32[8]{0:T(128)S(1)}, u32[]{:S(2)}, u32[]{:S(2)}) collective-permute-start(s32[8]{0:T(128)S(1)} %get-tuple-element.43), channel_id=1, source_target_pairs={{0,8},{4,12},{8,0},{12,4},{16,24},{20,28},{24,16},{28,20},{1,9},{5... | collective-permute-start | bytes 104 | tf_op jit(solution)/shard_map/ppermute | solution.py:24
  10.0 3.3 %fusion.2.q_ref = bf16[512,1024]{1,0:T(8,128)(2,1)S(1)} fusion(bf16[512,1024]{1,0:T(8,128)(2,1)} %refs_0_.3, bf16[1024,3072]{1,0:T(8,128)(2,1)} %param.5), kind=kOutput, calls=%fused_computation.12 | convolution fusion | flops 1074266112 | bytes 4194304 | tf_op jit(solution)/shard_map/dot_general | solution.py:180
  13.3 0.7 copy-done.2
  14.1 3.7 %convolution_convert_fusion.3.refs_0_.refs_4_ = bf16[512,2048]{1,0:T(8,128)(2,1)} fusion(bf16[512,1024]{1,0:T(8,128)(2,1)S(1)} %copy-done.1, bf16[1024,3072]{1,0:T(8,128)(2,1)S(1)} %copy-done.2), kind=kOutput, calls=%fused_computation.3 | convolution fusion | flops 2148532224 | bytes 7340032 | tf_op jit(solution)/shard_map/dot_general | solution.py:180
  17.8 9.3 %collective-permute-done.4.refs_2_ = bf16[512,1024]{1,0:T(8,128)(2,1)} collective-permute-done((bf16[512,1024]{1,0:T(8,128)(2,1)}, bf16[512,1024]{1,0:T(8,128)(2,1)}, u32[]{:S(2)}, u32[]{:S(2)}) %collective-permute-start.4) | collective-permute-done | bytes 1048608 | tf_op jit(solution)/shard_map/ppermute | solution.py:24
  27.5 2.5 %collective-permute-done.5.refs_3_ = bf16[512,1024]{1,0:T(8,128)(2,1)S(1)} collective-permute-done((bf16[512,1024]{1,0:T(8,128)(2,1)}, bf16[512,1024]{1,0:T(8,128)(2,1)S(1)}, u32[]{:S(2)}, u32[]{:S(2)}) %collective-permute-start.5) | collective-permute-done | bytes 1048608 | tf_op jit(solution)/shard_map/ppermute | solution.py:24
  30.0 3.4 %shard_map.46 = (bf16[256,1024]{1,0:T(8,128)(2,1)S(1)}, bf16[256,1024]{1,0:T(8,128)(2,1)S(1)}, bf16[256,1024]{1,0:T(8,128)(2,1)S(1)}) custom-call(s32[12]{0:T(128)S(1)} %pad_add_fusion.index_ref, bf16[512,1024]{1,0:T(8,128)(2,1)S(1)} %copy-done.1, bf16[512,1024]{1,0:T(8,128)(2,1)S(1)} %collective-permute-done.3.refs_1_, ...), custom_call_target="tpu_custom_call" | custom-call | bytes 3145728 | tf_op jit(solution)/shard_map/pallas_call | solution.py:68
  33.3 3.7 %convolution_convert_fusion.2.refs_1_.refs_5_ = bf16[512,2048]{1,0:T(8,128)(2,1)} fusion(bf16[512,1024]{1,0:T(8,128)(2,1)S(1)} %collective-permute-done.3.refs_1_, bf16[1024,3072]{1,0:T(8,128)(2,1)S(1)} %copy-done.2), kind=kOutput, calls=%fused_computation.2 | convolution fusion | flops 2148532224 | bytes 7340032 | tf_op jit(solution)/shard_map/dot_general | solution.py:180
  37.0 4.9 %convolution_convert_fusion.1.refs_2_.refs_6_ = bf16[512,2048]{1,0:T(8,128)(2,1)} fusion(bf16[512,1024]{1,0:T(8,128)(2,1)} %collective-permute-done.4.refs_2_, bf16[1024,3072]{1,0:T(8,128)(2,1)S(1)} %copy-done.2), kind=kOutput, calls=%fused_computation.1 | convolution fusion | flops 2148532224 | bytes 7340032 | tf_op jit(solution)/shard_map/dot_general | solution.py:180
  42.0 1.9 %collective-permute-start.6 = (bf16[256,1024]{1,0:T(8,128)(2,1)S(1)}, bf16[256,1024]{1,0:T(8,128)(2,1)S(1)}, u32[]{:S(2)}, u32[]{:S(2)}) collective-permute-start(bf16[256,1024]{1,0:T(8,128)(2,1)S(1)} %get-tuple-element.27), channel_id=1, source_target_pairs={{0,4},{4,0},{8,12},{12,8},{16,20},{20,16},{24,28},{28,24},{1,5},{5... | collective-permute-start | bytes 1572872 | tf_op jit(solution)/shard_map/ppermute | solution.py:24
  43.8 1.0 collective-permute-start.7
  44.8 2.4 %collective-permute-start.8 = (bf16[256,1024]{1,0:T(8,128)(2,1)S(1)}, bf16[256,1024]{1,0:T(8,128)(2,1)S(1)}, u32[]{:S(2)}, u32[]{:S(2)}) collective-permute-start(bf16[256,1024]{1,0:T(8,128)(2,1)S(1)} %get-tuple-element.29), channel_id=1, source_target_pairs={{0,16},{4,20},{8,24},{12,28},{16,0},{20,4},{24,8},{28,12},{1,17},{... | collective-permute-start | bytes 1572872 | tf_op jit(solution)/shard_map/ppermute | solution.py:24
  47.2 3.8 %convolution_convert_fusion.refs_3_.refs_7_ = bf16[512,2048]{1,0:T(8,128)(2,1)} fusion(bf16[512,1024]{1,0:T(8,128)(2,1)S(1)} %collective-permute-done.5.refs_3_, bf16[1024,3072]{1,0:T(8,128)(2,1)S(1)} %copy-done.2), kind=kOutput, calls=%fused_computation | convolution fusion | flops 2148532224 | bytes 7340032 | tf_op jit(solution)/shard_map/dot_general | solution.py:180
  50.9 4.6 %collective-permute-done.6 = bf16[256,1024]{1,0:T(8,128)(2,1)S(1)} collective-permute-done((bf16[256,1024]{1,0:T(8,128)(2,1)S(1)}, bf16[256,1024]{1,0:T(8,128)(2,1)S(1)}, u32[]{:S(2)}, u32[]{:S(2)}) %collective-permute-start.6) | collective-permute-done | bytes 524320 | tf_op jit(solution)/shard_map/ppermute | solution.py:24
  55.6 12.5 %collective-permute-done.7 = bf16[256,1024]{1,0:T(8,128)(2,1)S(1)} collective-permute-done((bf16[256,1024]{1,0:T(8,128)(2,1)S(1)}, bf16[256,1024]{1,0:T(8,128)(2,1)S(1)}, u32[]{:S(2)}, u32[]{:S(2)}) %collective-permute-start.7) | collective-permute-done | bytes 524320 | tf_op jit(solution)/shard_map/ppermute | solution.py:24
  68.1 2.3 %collective-permute-done.8 = bf16[256,1024]{1,0:T(8,128)(2,1)S(1)} collective-permute-done((bf16[256,1024]{1,0:T(8,128)(2,1)S(1)}, bf16[256,1024]{1,0:T(8,128)(2,1)S(1)}, u32[]{:S(2)}, u32[]{:S(2)}) %collective-permute-start.8) | collective-permute-done | bytes 524320 | tf_op jit(solution)/shard_map/ppermute | solution.py:24
  70.4 3.0 %shard_map.48 = (bf16[256,1024]{1,0:T(8,128)(2,1)S(1)}, bf16[256,1024]{1,0:T(8,128)(2,1)S(1)}, bf16[256,1024]{1,0:T(8,128)(2,1)S(1)}) custom-call(s32[12]{0:T(128)S(1)} %pad_add_fusion.1.index_ref, bf16[512,1024]{1,0:T(8,128)(2,1)S(1)} %copy-done.1, bf16[512,1024]{1,0:T(8,128)(2,1)S(1)} %collective-permute-done.3.refs_1_, ...), custom_call_target="tpu_custom_call" | custom-call | bytes 3145728 | tf_op jit(solution)/shard_map/pallas_call | solution.py:68
  73.3 1.2 collective-permute-start.9
  75.0 1.9 %collective-permute-start.11 = (bf16[256,1024]{1,0:T(8,128)(2,1)S(1)}, bf16[256,1024]{1,0:T(8,128)(2,1)S(1)}, u32[]{:S(2)}, u32[]{:S(2)}) collective-permute-start(bf16[256,1024]{1,0:T(8,128)(2,1)S(1)} %get-tuple-element.36), channel_id=1, source_target_pairs={{0,16},{4,20},{8,24},{12,28},{16,0},{20,4},{24,8},{28,12},{1,17},{... | collective-permute-start | bytes 1572872 | tf_op jit(solution)/shard_map/ppermute | solution.py:24
  76.9 1.3 convolution_convert_fusion.9.refs_8_.refs_11_
  78.2 1.3 convolution_convert_fusion.8.refs_9_.refs_12_
  79.5 1.3 convolution_convert_fusion.7.refs_10_.refs_13_
  80.8 20.7 %shard_map.47 = bf16[256,1024]{1,0:T(8,128)(2,1)S(1)} custom-call(s32[40]{0:T(128)S(1)} %reshape.6.index_ref, bf16[512,1024]{1,0:T(8,128)(2,1)S(1)} %fusion.2.q_ref, bf16[512,2048]{1,0:T(8,128)(2,1)} %convolution_convert_fusion.3.refs_0_.refs_4_, bf16[512,2048]{1,0:T(8,128)(2,1)} %convolution_convert_fusion.2.refs_1_.refs_5_, ...), custom_call_target="tpu_custom_call" | custom-call | flops 6979321856 | bytes 8388608 | tf_op jit(solution)/shard_map/pallas_call | solution.py:154
  102.3 2.3 %convolution_convert_fusion.6.refs_8_.refs_11_ = bf16[256,2048]{1,0:T(8,128)(2,1)S(1)} fusion(bf16[256,1024]{1,0:T(8,128)(2,1)} %collective-permute-done.9, bf16[1024,3072]{1,0:T(8,128)(2,1)S(1)} %copy-done.2), kind=kOutput, calls=%fused_computation.6 | convolution fusion | flops 1074266112 | bytes 5767168 | tf_op jit(solution)/shard_map/dot_general | solution.py:180
  104.7 1.3 convolution_convert_fusion.5.refs_9_.refs_12_
  105.9 1.3 convolution_convert_fusion.4.refs_10_.refs_13_
  107.2 20.8 %shard_map.49 = bf16[256,1024]{1,0:T(8,128)(2,1)S(1)} custom-call(s32[40]{0:T(128)S(1)} %reshape.7.index_ref, bf16[512,1024]{1,0:T(8,128)(2,1)S(1)} %fusion.2.q_ref, bf16[512,2048]{1,0:T(8,128)(2,1)} %convolution_convert_fusion.3.refs_0_.refs_4_, bf16[512,2048]{1,0:T(8,128)(2,1)} %convolution_convert_fusion.2.refs_1_.refs_5_, ...), custom_call_target="tpu_custom_call" | custom-call | flops 6979321856 | bytes 8388608 | tf_op jit(solution)/shard_map/pallas_call | solution.py:154
  128.7 1.0 pad_maximum_fusion
  (30 shorter events, 3.2 us)
Async XLA Ops:
  0.0 101.5 %copy-start = (bf16[1024,1024]{1,0:T(8,128)(2,1)S(1)}, bf16[1024,1024]{1,0:T(8,128)(2,1)}, u32[]{:S(2)}) copy-start(bf16[1024,1024]{1,0:T(8,128)(2,1)} %param.6) | copy-start | bytes 6291460
  0.0 27.5 %collective-permute-start.3 = (bf16[512,1024]{1,0:T(8,128)(2,1)}, bf16[512,1024]{1,0:T(8,128)(2,1)S(1)}, u32[]{:S(2)}, u32[]{:S(2)}) collective-permute-start(bf16[512,1024]{1,0:T(8,128)(2,1)} %refs_0_.3), channel_id=1, source_target_pairs={{0,1},{1,0},{2,3},{3,2},{4,5},{5,4},{6,7},{7,6},{8,9},{9,8},{10,11... | collective-permute-start | bytes 3145736 | tf_op jit(solution)/shard_map/ppermute | solution.py:24
  0.5 26.6 %collective-permute-start.4 = (bf16[512,1024]{1,0:T(8,128)(2,1)}, bf16[512,1024]{1,0:T(8,128)(2,1)}, u32[]{:S(2)}, u32[]{:S(2)}) collective-permute-start(bf16[512,1024]{1,0:T(8,128)(2,1)} %refs_0_.3), channel_id=1, source_target_pairs={{0,2},{1,3},{2,0},{3,1},{4,6},{5,7},{6,4},{7,5},{8,10},{9,11},{10,... | collective-permute-start | bytes 3145736 | tf_op jit(solution)/shard_map/ppermute | solution.py:24
  3.8 14.0 %collective-permute-start.2 = (s32[8]{0:T(128)S(1)}, s32[8]{0:T(128)S(1)}, u32[]{:S(2)}, u32[]{:S(2)}) collective-permute-start(s32[8]{0:T(128)S(1)} %get-tuple-element.42), channel_id=1, source_target_pairs={{0,16},{4,20},{8,24},{12,28},{16,0},{20,4},{24,8},{28,12},{1,17},{... | collective-permute-start | bytes 104 | tf_op jit(solution)/shard_map/ppermute | solution.py:24
  6.5 20.7 %collective-permute-start = (s32[8]{0:T(128)S(1)}, s32[8]{0:T(128)S(1)}, u32[]{:S(2)}, u32[]{:S(2)}) collective-permute-start(s32[8]{0:T(128)S(1)} %get-tuple-element.41), channel_id=1, source_target_pairs={{0,4},{4,0},{8,12},{12,8},{16,20},{20,16},{24,28},{28,24},{1,5},{5... | collective-permute-start | bytes 104 | tf_op jit(solution)/shard_map/ppermute | solution.py:24
  8.0 19.2 %collective-permute-start.1 = (s32[8]{0:T(128)S(1)}, s32[8]{0:T(128)S(1)}, u32[]{:S(2)}, u32[]{:S(2)}) collective-permute-start(s32[8]{0:T(128)S(1)} %get-tuple-element.43), channel_id=1, source_target_pairs={{0,8},{4,12},{8,0},{12,4},{16,24},{20,28},{24,16},{28,20},{1,9},{5... | collective-permute-start | bytes 104 | tf_op jit(solution)/shard_map/ppermute | solution.py:24
  10.0 3.3 %copy-start.1 = (bf16[512,1024]{1,0:T(8,128)(2,1)S(1)}, bf16[512,1024]{1,0:T(8,128)(2,1)}, u32[]{:S(2)}) copy-start(bf16[512,1024]{1,0:T(8,128)(2,1)} %refs_0_.3) | copy-start | bytes 3145732
  10.0 4.1 %copy-start.2 = (bf16[1024,3072]{1,0:T(8,128)(2,1)S(1)}, bf16[1024,3072]{1,0:T(8,128)(2,1)}, u32[]{:S(2)}) copy-start(bf16[1024,3072]{1,0:T(8,128)(2,1)} %param.5) | copy-start | bytes 18874372
  27.1 2.9 %collective-permute-start.5 = (bf16[512,1024]{1,0:T(8,128)(2,1)}, bf16[512,1024]{1,0:T(8,128)(2,1)S(1)}, u32[]{:S(2)}, u32[]{:S(2)}) collective-permute-start(bf16[512,1024]{1,0:T(8,128)(2,1)} %collective-permute-done.4.refs_2_), channel_id=1, source_target_pairs={{0,1},{1,0},{2,3},{3,2},{4,5},{5,4},{6,7},{7,6},{8,9},{9,8},{10,11... | collective-permute-start | bytes 3145736 | tf_op jit(solution)/shard_map/ppermute | solution.py:24
  42.0 13.6 %collective-permute-start.6 = (bf16[256,1024]{1,0:T(8,128)(2,1)S(1)}, bf16[256,1024]{1,0:T(8,128)(2,1)S(1)}, u32[]{:S(2)}, u32[]{:S(2)}) collective-permute-start(bf16[256,1024]{1,0:T(8,128)(2,1)S(1)} %get-tuple-element.27), channel_id=1, source_target_pairs={{0,4},{4,0},{8,12},{12,8},{16,20},{20,16},{24,28},{28,24},{1,5},{5... | collective-permute-start | bytes 1572872 | tf_op jit(solution)/shard_map/ppermute | solution.py:24
  43.8 24.3 %collective-permute-start.7 = (bf16[256,1024]{1,0:T(8,128)(2,1)S(1)}, bf16[256,1024]{1,0:T(8,128)(2,1)S(1)}, u32[]{:S(2)}, u32[]{:S(2)}) collective-permute-start(bf16[256,1024]{1,0:T(8,128)(2,1)S(1)} %get-tuple-element.28), channel_id=1, source_target_pairs={{0,8},{4,12},{8,0},{12,4},{16,24},{20,28},{24,16},{28,20},{1,9},{5... | collective-permute-start | bytes 1572872 | tf_op jit(solution)/shard_map/ppermute | solution.py:24
  44.8 25.6 %collective-permute-start.8 = (bf16[256,1024]{1,0:T(8,128)(2,1)S(1)}, bf16[256,1024]{1,0:T(8,128)(2,1)S(1)}, u32[]{:S(2)}, u32[]{:S(2)}) collective-permute-start(bf16[256,1024]{1,0:T(8,128)(2,1)S(1)} %get-tuple-element.29), channel_id=1, source_target_pairs={{0,16},{4,20},{8,24},{12,28},{16,0},{20,4},{24,8},{28,12},{1,17},{... | collective-permute-start | bytes 1572872 | tf_op jit(solution)/shard_map/ppermute | solution.py:24
  73.3 28.9 %collective-permute-start.9 = (bf16[256,1024]{1,0:T(8,128)(2,1)S(1)}, bf16[256,1024]{1,0:T(8,128)(2,1)}, u32[]{:S(2)}, u32[]{:S(2)}) collective-permute-start(bf16[256,1024]{1,0:T(8,128)(2,1)S(1)} %get-tuple-element.34), channel_id=1, source_target_pairs={{0,4},{4,0},{8,12},{12,8},{16,20},{20,16},{24,28},{28,24},{1,5},{5... | collective-permute-start | bytes 1572872 | tf_op jit(solution)/shard_map/ppermute | solution.py:24
  74.5 30.1 %collective-permute-start.10 = (bf16[256,1024]{1,0:T(8,128)(2,1)S(1)}, bf16[256,1024]{1,0:T(8,128)(2,1)S(1)}, u32[]{:S(2)}, u32[]{:S(2)}) collective-permute-start(bf16[256,1024]{1,0:T(8,128)(2,1)S(1)} %get-tuple-element.35), channel_id=1, source_target_pairs={{0,8},{4,12},{8,0},{12,4},{16,24},{20,28},{24,16},{28,20},{1,9},{5... | collective-permute-start | bytes 1572872 | tf_op jit(solution)/shard_map/ppermute | solution.py:24
  75.0 30.9 %collective-permute-start.11 = (bf16[256,1024]{1,0:T(8,128)(2,1)S(1)}, bf16[256,1024]{1,0:T(8,128)(2,1)S(1)}, u32[]{:S(2)}, u32[]{:S(2)}) collective-permute-start(bf16[256,1024]{1,0:T(8,128)(2,1)S(1)} %get-tuple-element.36), channel_id=1, source_target_pairs={{0,16},{4,20},{8,24},{12,28},{16,0},{20,4},{24,8},{28,12},{1,17},{... | collective-permute-start | bytes 1572872 | tf_op jit(solution)/shard_map/ppermute | solution.py:24

commit v5 on v4

--- a/solution.py
+++ b/solution.py
@@ -204,10 +204,9 @@
         if part == 1:
             index, arrived[0] = lax.optimization_barrier((index, arrived[0]))
         picked = pick_blocks(shards, index)
-        if part == 0:
-            picked, later = lax.optimization_barrier((picked, shards[1:]))
         arrived.append([exchange(rows, "seg", 1 << j) for j, rows in enumerate(picked)])
         if part == 0:
+            arrived[0][0], later = lax.optimization_barrier((arrived[0][0], shards[1:]))
             own += [project(shard, w_kv) for shard in later]
     mixed = []
     for part in range(PARTS):

time: 131 us -> 129 us (0.985)
  waiting for transfers between devices: 31.2 us -> 21 us
  matrix products: 29.5 us -> 35.1 us
  local copies, waits for them, and re-layouts: 1.41 us -> 3.24 us
    ppermute x12, waiting for transfers between devices: 31.2 us -> 21 us  [exchange(): return lax.ppermute(value, axis, pairs)]
    dot_general x13, matrix products: 29.5 us -> 35.1 us  [project(): jnp.dot(rows, weights, preferred_element_type=jnp.float32)]
    unnamed x6 -> x20, local copies, waits for them, and re-layouts: 0.76 us -> 2.59 us
  transfers between devices with their start and end apart: 12 -> 12, of which waited for: 5 -> 5; matrix products, arithmetic and copies ran while one was open for 16% -> 27% of each run, Pallas kernels for 16% -> 16%
where the time goes in v5:
time: 129 us; the launch traced here: 128 us
  Pallas kernels  47.5 us (37%)
  matrix products  35.1 us (27%)
  waiting for transfers between devices  21 us (16%)
  starting transfers between devices  18.7 us (14%)
  local copies, waits for them, and re-layouts  3.24 us (3%)
  other arithmetic  2.01 us (2%)
    pallas_call x2, Pallas kernels, attend(): pl.pallas_call(functools.partial(attend_body, unroll, len(own)), grid_spe...  41.5 us
    dot_general x13, matrix products, project(): jnp.dot(rows, weights, preferred_element_type=jnp.float32)  35.1 us
    ppermute x12, waiting for transfers between devices, exchange(): return lax.ppermute(value, axis, pairs)  21 us
    ppermute x12, starting transfers between devices, exchange(): return lax.ppermute(value, axis, pairs)  18.7 us
    pallas_call x2, Pallas kernels, pick_blocks(): pl.pallas_call(pick_body, grid_spec=pltpu.PrefetchScalarGridSpec(num_scal...  5.95 us
    unnamed x20, local copies, waits for them, and re-layouts  2.59 us
  transfers between devices with their start and end apart: 12, of which 5 were waited for; matrix products, arithmetic and copies ran while one was open for 27% of the time, Pallas kernels for 16%

profile of v5, /device:TPU:0, one launch (start us, length us, event | category | flops | bytes accessed | tf_op | source)
XLA Modules:
  0.0 127.7 jit_solution(15339970525160381530)
XLA Ops:
  0.0 2.9 %collective-permute-start.4 = (bf16[512,1024]{1,0:T(8,128)(2,1)}, bf16[512,1024]{1,0:T(8,128)(2,1)}, u32[]{:S(2)}, u32[]{:S(2)}) collective-permute-start(bf16[512,1024]{1,0:T(8,128)(2,1)} %refs_0_.3), channel_id=1, source_target_pairs={{0,2},{1,3},{2,0},{3,1},{4,6},{5,7},{6,4},{7,5},{8,10},{9,11},{10,... | collective-permute-start | bytes 3145736 | tf_op jit(solution)/shard_map/ppermute | solution.py:24
  2.9 0.8 fusion.8
  3.7 2.7 %collective-permute-start.2 = (s32[8]{0:T(128)S(1)}, s32[8]{0:T(128)S(1)}, u32[]{:S(2)}, u32[]{:S(2)}) collective-permute-start(s32[8]{0:T(128)S(1)} %get-tuple-element.38), channel_id=1, source_target_pairs={{0,16},{4,20},{8,24},{12,28},{16,0},{20,4},{24,8},{28,12},{1,17},{... | collective-permute-start | bytes 104 | tf_op jit(solution)/shard_map/ppermute | solution.py:24
  6.4 1.5 %collective-permute-start = (s32[8]{0:T(128)S(1)}, s32[8]{0:T(128)S(1)}, u32[]{:S(2)}, u32[]{:S(2)}) collective-permute-start(s32[8]{0:T(128)S(1)} %get-tuple-element.37), channel_id=1, source_target_pairs={{0,4},{4,0},{8,12},{12,8},{16,20},{20,16},{24,28},{28,24},{1,5},{5... | collective-permute-start | bytes 104 | tf_op jit(solution)/shard_map/ppermute | solution.py:24
  7.9 1.6 %collective-permute-start.1 = (s32[8]{0:T(128)S(1)}, s32[8]{0:T(128)S(1)}, u32[]{:S(2)}, u32[]{:S(2)}) collective-permute-start(s32[8]{0:T(128)S(1)} %get-tuple-element.39), channel_id=1, source_target_pairs={{0,8},{4,12},{8,0},{12,4},{16,24},{20,28},{24,16},{28,20},{1,9},{5... | collective-permute-start | bytes 104 | tf_op jit(solution)/shard_map/ppermute | solution.py:24
  9.5 6.2 %convolution_convert_fusion.3.refs_0_.refs_4_ = bf16[512,2048]{1,0:T(8,128)(2,1)} fusion(bf16[512,1024]{1,0:T(8,128)(2,1)} %refs_0_.3, bf16[1024,3072]{1,0:T(8,128)(2,1)} %param.5), kind=kOutput, calls=%fused_computation.3 | convolution fusion | flops 2148532224 | bytes 7340032 | tf_op jit(solution)/shard_map/dot_general | solution.py:180
  15.7 10.7 %collective-permute-done.4.refs_2_ = bf16[512,1024]{1,0:T(8,128)(2,1)} collective-permute-done((bf16[512,1024]{1,0:T(8,128)(2,1)}, bf16[512,1024]{1,0:T(8,128)(2,1)}, u32[]{:S(2)}, u32[]{:S(2)}) %collective-permute-start.4) | collective-permute-done | bytes 1048608 | tf_op jit(solution)/shard_map/ppermute | solution.py:24
  26.8 2.5 %collective-permute-done.5.refs_3_ = bf16[512,1024]{1,0:T(8,128)(2,1)S(1)} collective-permute-done((bf16[512,1024]{1,0:T(8,128)(2,1)}, bf16[512,1024]{1,0:T(8,128)(2,1)S(1)}, u32[]{:S(2)}, u32[]{:S(2)}) %collective-permute-start.5) | collective-permute-done | bytes 1048608 | tf_op jit(solution)/shard_map/ppermute | solution.py:24
  29.3 3.4 %shard_map.46 = (bf16[256,1024]{1,0:T(8,128)(2,1)}, bf16[256,1024]{1,0:T(8,128)(2,1)S(1)}, bf16[256,1024]{1,0:T(8,128)(2,1)S(1)}) custom-call(s32[12]{0:T(128)S(1)} %pad_add_fusion.index_ref, bf16[512,1024]{1,0:T(8,128)(2,1)S(1)} %copy-done.1, bf16[512,1024]{1,0:T(8,128)(2,1)} %collective-permute-done.3.refs_1_, ...), custom_call_target="tpu_custom_call" | custom-call | bytes 3145728 | tf_op jit(solution)/shard_map/pallas_call | solution.py:68
  32.7 1.0 copy-done.2
  34.4 0.8 copy-done.6
  35.2 1.8 %collective-permute-start.6 = (bf16[256,1024]{1,0:T(8,128)(2,1)}, bf16[256,1024]{1,0:T(8,128)(2,1)}, u32[]{:S(2)}, u32[]{:S(2)}) collective-permute-start(bf16[256,1024]{1,0:T(8,128)(2,1)} %get-tuple-element.19), channel_id=1, source_target_pairs={{0,4},{4,0},{8,12},{12,8},{16,20},{20,16},{24,28},{28,24},{1,5},{5... | collective-permute-start | bytes 1572872 | tf_op jit(solution)/shard_map/ppermute | solution.py:24
  37.4 2.9 %fusion.2.q_ref = bf16[512,1024]{1,0:T(8,128)(2,1)S(1)} fusion(bf16[512,1024]{1,0:T(8,128)(2,1)S(1)} %copy-done.1, bf16[1024,3072]{1,0:T(8,128)(2,1)} %param.5), kind=kOutput, calls=%fused_computation.12 | convolution fusion | flops 1074266112 | bytes 4194304 | tf_op jit(solution)/shard_map/dot_general | solution.py:180
  40.5 1.6 %collective-permute-start.7 = (bf16[256,1024]{1,0:T(8,128)(2,1)S(1)}, bf16[256,1024]{1,0:T(8,128)(2,1)S(1)}, u32[]{:S(2)}, u32[]{:S(2)}) collective-permute-start(bf16[256,1024]{1,0:T(8,128)(2,1)S(1)} %copy-done.7), channel_id=1, source_target_pairs={{0,8},{4,12},{8,0},{12,4},{16,24},{20,28},{24,16},{28,20},{1,9},{5... | collective-permute-start | bytes 1572872 | tf_op jit(solution)/shard_map/ppermute | solution.py:24
  42.1 3.0 %collective-permute-start.8 = (bf16[256,1024]{1,0:T(8,128)(2,1)S(1)}, bf16[256,1024]{1,0:T(8,128)(2,1)S(1)}, u32[]{:S(2)}, u32[]{:S(2)}) collective-permute-start(bf16[256,1024]{1,0:T(8,128)(2,1)S(1)} %copy-done.5), channel_id=1, source_target_pairs={{0,16},{4,20},{8,24},{12,28},{16,0},{20,4},{24,8},{28,12},{1,17},{... | collective-permute-start | bytes 1572872 | tf_op jit(solution)/shard_map/ppermute | solution.py:24
  45.1 4.5 %collective-permute-done.6 = bf16[256,1024]{1,0:T(8,128)(2,1)} collective-permute-done((bf16[256,1024]{1,0:T(8,128)(2,1)}, bf16[256,1024]{1,0:T(8,128)(2,1)}, u32[]{:S(2)}, u32[]{:S(2)}) %collective-permute-start.6) | collective-permute-done | bytes 524320 | tf_op jit(solution)/shard_map/ppermute | solution.py:24
  49.7 6.2 %convolution_convert_fusion.2.refs_1_.refs_5_ = bf16[512,2048]{1,0:T(8,128)(2,1)} fusion(bf16[512,1024]{1,0:T(8,128)(2,1)} %collective-permute-done.3.refs_1_, bf16[1024,3072]{1,0:T(8,128)(2,1)} %param.5), kind=kOutput, calls=%fused_computation.2 | convolution fusion | flops 2148532224 | bytes 7340032 | tf_op jit(solution)/shard_map/dot_general | solution.py:180
  55.9 5.0 %convolution_convert_fusion.1.refs_2_.refs_6_ = bf16[512,2048]{1,0:T(8,128)(2,1)} fusion(bf16[512,1024]{1,0:T(8,128)(2,1)} %collective-permute-done.4.refs_2_, bf16[1024,3072]{1,0:T(8,128)(2,1)S(1)} %bitcast.22), kind=kOutput, calls=%fused_computation.1 | convolution fusion | flops 2148532224 | bytes 7340032 | tf_op jit(solution)/shard_map/dot_general | solution.py:180
  60.9 3.7 %convolution_convert_fusion.refs_3_.refs_7_ = bf16[512,2048]{1,0:T(8,128)(2,1)} fusion(bf16[512,1024]{1,0:T(8,128)(2,1)S(1)} %copy-done.3, bf16[1024,3072]{1,0:T(8,128)(2,1)S(1)} %bitcast.22), kind=kOutput, calls=%fused_computation | convolution fusion | flops 2148532224 | bytes 7340032 | tf_op jit(solution)/shard_map/dot_general | solution.py:180
  65.4 2.5 %collective-permute-done.8 = bf16[256,1024]{1,0:T(8,128)(2,1)S(1)} collective-permute-done((bf16[256,1024]{1,0:T(8,128)(2,1)S(1)}, bf16[256,1024]{1,0:T(8,128)(2,1)S(1)}, u32[]{:S(2)}, u32[]{:S(2)}) %collective-permute-start.8) | collective-permute-done | bytes 524320 | tf_op jit(solution)/shard_map/ppermute | solution.py:24
  67.8 2.6 %shard_map.48 = (bf16[256,1024]{1,0:T(8,128)(2,1)S(1)}, bf16[256,1024]{1,0:T(8,128)(2,1)S(1)}, bf16[256,1024]{1,0:T(8,128)(2,1)S(1)}) custom-call(s32[12]{0:T(128)S(1)} %pad_add_fusion.1.index_ref, bf16[512,1024]{1,0:T(8,128)(2,1)S(1)} %copy-done.1, bf16[512,1024]{1,0:T(8,128)(2,1)} %collective-permute-done.3.refs_1_, ...), custom_call_target="tpu_custom_call" | custom-call | bytes 3145728 | tf_op jit(solution)/shard_map/pallas_call | solution.py:68
  70.4 1.0 collective-permute-start.9
  71.4 2.7 %collective-permute-start.11 = (bf16[256,1024]{1,0:T(8,128)(2,1)S(1)}, bf16[256,1024]{1,0:T(8,128)(2,1)S(1)}, u32[]{:S(2)}, u32[]{:S(2)}) collective-permute-start(bf16[256,1024]{1,0:T(8,128)(2,1)S(1)} %get-tuple-element.32), channel_id=1, source_target_pairs={{0,16},{4,20},{8,24},{12,28},{16,0},{20,4},{24,8},{28,12},{1,17},{... | collective-permute-start | bytes 1572872 | tf_op jit(solution)/shard_map/ppermute | solution.py:24
  74.0 2.3 %convolution_convert_fusion.9.refs_8_.refs_11_ = bf16[256,2048]{1,0:T(8,128)(2,1)S(1)} fusion(bf16[256,1024]{1,0:T(8,128)(2,1)} %collective-permute-done.6, bf16[1024,3072]{1,0:T(8,128)(2,1)S(1)} %bitcast.22), kind=kOutput, calls=%fused_computation.9 | convolution fusion | flops 1074266112 | bytes 5767168 | tf_op jit(solution)/shard_map/dot_general | solution.py:180
  76.3 1.3 convolution_convert_fusion.8.refs_9_.refs_12_
  77.6 1.3 convolution_convert_fusion.7.refs_10_.refs_13_
  78.9 20.7 %shard_map.47 = bf16[256,1024]{1,0:T(8,128)(2,1)S(1)} custom-call(s32[40]{0:T(128)S(1)} %reshape.6.index_ref, bf16[512,1024]{1,0:T(8,128)(2,1)S(1)} %fusion.2.q_ref, bf16[512,2048]{1,0:T(8,128)(2,1)} %convolution_convert_fusion.3.refs_0_.refs_4_, bf16[512,2048]{1,0:T(8,128)(2,1)} %convolution_convert_fusion.2.refs_1_.refs_5_, ...), custom_call_target="tpu_custom_call" | custom-call | flops 6979321856 | bytes 8388608 | tf_op jit(solution)/shard_map/pallas_call | solution.py:154
  100.3 2.3 %convolution_convert_fusion.6.refs_8_.refs_11_ = bf16[256,2048]{1,0:T(8,128)(2,1)S(1)} fusion(bf16[256,1024]{1,0:T(8,128)(2,1)} %collective-permute-done.9, bf16[1024,3072]{1,0:T(8,128)(2,1)S(1)} %bitcast.22), kind=kOutput, calls=%fused_computation.6 | convolution fusion | flops 1074266112 | bytes 5767168 | tf_op jit(solution)/shard_map/dot_general | solution.py:180
  102.7 1.3 convolution_convert_fusion.5.refs_9_.refs_12_
  103.9 1.3 convolution_convert_fusion.4.refs_10_.refs_13_
  105.2 20.8 %shard_map.49 = bf16[256,1024]{1,0:T(8,128)(2,1)S(1)} custom-call(s32[40]{0:T(128)S(1)} %reshape.7.index_ref, bf16[512,1024]{1,0:T(8,128)(2,1)S(1)} %fusion.2.q_ref, bf16[512,2048]{1,0:T(8,128)(2,1)} %convolution_convert_fusion.3.refs_0_.refs_4_, bf16[512,2048]{1,0:T(8,128)(2,1)} %convolution_convert_fusion.2.refs_1_.refs_5_, ...), custom_call_target="tpu_custom_call" | custom-call | flops 6979321856 | bytes 8388608 | tf_op jit(solution)/shard_map/pallas_call | solution.py:154
  126.7 1.0 pad_maximum_fusion
  (45 shorter events, 3.8 us)
Async XLA Ops:
  0.0 99.6 %copy-start = (bf16[1024,1024]{1,0:T(8,128)(2,1)S(1)}, bf16[1024,1024]{1,0:T(8,128)(2,1)}, u32[]{:S(2)}) copy-start(bf16[1024,1024]{1,0:T(8,128)(2,1)} %param.6) | copy-start | bytes 6291460
  0.0 26.4 %collective-permute-start.4 = (bf16[512,1024]{1,0:T(8,128)(2,1)}, bf16[512,1024]{1,0:T(8,128)(2,1)}, u32[]{:S(2)}, u32[]{:S(2)}) collective-permute-start(bf16[512,1024]{1,0:T(8,128)(2,1)} %refs_0_.3), channel_id=1, source_target_pairs={{0,2},{1,3},{2,0},{3,1},{4,6},{5,7},{6,4},{7,5},{8,10},{9,11},{10,... | collective-permute-start | bytes 3145736 | tf_op jit(solution)/shard_map/ppermute | solution.py:24
  2.9 23.8 %collective-permute-start.3 = (bf16[512,1024]{1,0:T(8,128)(2,1)}, bf16[512,1024]{1,0:T(8,128)(2,1)}, u32[]{:S(2)}, u32[]{:S(2)}) collective-permute-start(bf16[512,1024]{1,0:T(8,128)(2,1)} %refs_0_.3), channel_id=1, source_target_pairs={{0,1},{1,0},{2,3},{3,2},{4,5},{5,4},{6,7},{7,6},{8,9},{9,8},{10,11... | collective-permute-start | bytes 3145736 | tf_op jit(solution)/shard_map/ppermute | solution.py:24
  3.7 22.7 %collective-permute-start.2 = (s32[8]{0:T(128)S(1)}, s32[8]{0:T(128)S(1)}, u32[]{:S(2)}, u32[]{:S(2)}) collective-permute-start(s32[8]{0:T(128)S(1)} %get-tuple-element.38), channel_id=1, source_target_pairs={{0,16},{4,20},{8,24},{12,28},{16,0},{20,4},{24,8},{28,12},{1,17},{... | collective-permute-start | bytes 104 | tf_op jit(solution)/shard_map/ppermute | solution.py:24
  6.4 20.1 %collective-permute-start = (s32[8]{0:T(128)S(1)}, s32[8]{0:T(128)S(1)}, u32[]{:S(2)}, u32[]{:S(2)}) collective-permute-start(s32[8]{0:T(128)S(1)} %get-tuple-element.37), channel_id=1, source_target_pairs={{0,4},{4,0},{8,12},{12,8},{16,20},{20,16},{24,28},{28,24},{1,5},{5... | collective-permute-start | bytes 104 | tf_op jit(solution)/shard_map/ppermute | solution.py:24
  7.9 21.4 %copy-start.1 = (bf16[512,1024]{1,0:T(8,128)(2,1)S(1)}, bf16[512,1024]{1,0:T(8,128)(2,1)}, u32[]{:S(2)}) copy-start(bf16[512,1024]{1,0:T(8,128)(2,1)} %refs_0_.3) | copy-start | bytes 3145732
  7.9 18.6 %collective-permute-start.1 = (s32[8]{0:T(128)S(1)}, s32[8]{0:T(128)S(1)}, u32[]{:S(2)}, u32[]{:S(2)}) collective-permute-start(s32[8]{0:T(128)S(1)} %get-tuple-element.39), channel_id=1, source_target_pairs={{0,8},{4,12},{8,0},{12,4},{16,24},{20,28},{24,16},{28,20},{1,9},{5... | collective-permute-start | bytes 104 | tf_op jit(solution)/shard_map/ppermute | solution.py:24
  26.4 2.9 %collective-permute-start.5 = (bf16[512,1024]{1,0:T(8,128)(2,1)}, bf16[512,1024]{1,0:T(8,128)(2,1)S(1)}, u32[]{:S(2)}, u32[]{:S(2)}) collective-permute-start(bf16[512,1024]{1,0:T(8,128)(2,1)} %collective-permute-done.4.refs_2_), channel_id=1, source_target_pairs={{0,1},{1,0},{2,3},{3,2},{4,5},{5,4},{6,7},{7,6},{8,9},{9,8},{10,11... | collective-permute-start | bytes 3145736 | tf_op jit(solution)/shard_map/ppermute | solution.py:24
  32.7 1.0 copy-start.2
  33.6 0.8 copy-start.4
  34.4 0.8 copy-start.6
  35.2 14.4 %collective-permute-start.6 = (bf16[256,1024]{1,0:T(8,128)(2,1)}, bf16[256,1024]{1,0:T(8,128)(2,1)}, u32[]{:S(2)}, u32[]{:S(2)}) collective-permute-start(bf16[256,1024]{1,0:T(8,128)(2,1)} %get-tuple-element.19), channel_id=1, source_target_pairs={{0,4},{4,0},{8,12},{12,8},{16,20},{20,16},{24,28},{28,24},{1,5},{5... | collective-permute-start | bytes 1572872 | tf_op jit(solution)/shard_map/ppermute | solution.py:24
  37.4 3.0 %copy-start.7 = (bf16[256,1024]{1,0:T(8,128)(2,1)S(1)}, bf16[256,1024]{1,0:T(8,128)(2,1)}, u32[]{:S(2)}) copy-start(bf16[256,1024]{1,0:T(8,128)(2,1)} %copy-done.6) | copy-start | bytes 1572868
  37.4 4.7 %copy-start.5 = (bf16[256,1024]{1,0:T(8,128)(2,1)S(1)}, bf16[256,1024]{1,0:T(8,128)(2,1)}, u32[]{:S(2)}) copy-start(bf16[256,1024]{1,0:T(8,128)(2,1)} %copy-done.4) | copy-start | bytes 1572868
  40.5 24.9 %collective-permute-start.7 = (bf16[256,1024]{1,0:T(8,128)(2,1)S(1)}, bf16[256,1024]{1,0:T(8,128)(2,1)S(1)}, u32[]{:S(2)}, u32[]{:S(2)}) collective-permute-start(bf16[256,1024]{1,0:T(8,128)(2,1)S(1)} %copy-done.7), channel_id=1, source_target_pairs={{0,8},{4,12},{8,0},{12,4},{16,24},{20,28},{24,16},{28,20},{1,9},{5... | collective-permute-start | bytes 1572872 | tf_op jit(solution)/shard_map/ppermute | solution.py:24
  42.1 13.8 %slice-start = ((s8[6291456]{0:T(1024)(128)(4,1)}), s8[4194304]{0:T(1024)(128)(4,1)S(1)}, s32[]{:S(2)}) async-start(s8[6291456]{0:T(1024)(128)(4,1)} %bitcast.21), calls=%async_computation | async-start | bytes 8388608
  42.1 13.8 %slice-start.1 = ((s8[6291456]{0:T(1024)(128)(4,1)}), s8[2097152]{0:T(1024)(128)(4,1)S(1)}, s32[]{:S(2)}) async-start(s8[6291456]{0:T(1024)(128)(4,1)} %bitcast.21), calls=%async_computation.1 | async-start | bytes 4194304
  42.1 25.8 %collective-permute-start.8 = (bf16[256,1024]{1,0:T(8,128)(2,1)S(1)}, bf16[256,1024]{1,0:T(8,128)(2,1)S(1)}, u32[]{:S(2)}, u32[]{:S(2)}) collective-permute-start(bf16[256,1024]{1,0:T(8,128)(2,1)S(1)} %copy-done.5), channel_id=1, source_target_pairs={{0,16},{4,20},{8,24},{12,28},{16,0},{20,4},{24,8},{28,12},{1,17},{... | collective-permute-start | bytes 1572872 | tf_op jit(solution)/shard_map/ppermute | solution.py:24
  55.9 5.0 %copy-start.3 = (bf16[512,1024]{1,0:T(8,128)(2,1)S(1)}, bf16[512,1024]{1,0:T(8,128)(2,1)}, u32[]{:S(2)}) copy-start(bf16[512,1024]{1,0:T(8,128)(2,1)} %copy-done.2) | copy-start | bytes 3145732
  70.4 29.9 %collective-permute-start.9 = (bf16[256,1024]{1,0:T(8,128)(2,1)S(1)}, bf16[256,1024]{1,0:T(8,128)(2,1)}, u32[]{:S(2)}, u32[]{:S(2)}) collective-permute-start(bf16[256,1024]{1,0:T(8,128)(2,1)S(1)} %get-tuple-element.30), channel_id=1, source_target_pairs={{0,4},{4,0},{8,12},{12,8},{16,20},{20,16},{24,28},{28,24},{1,5},{5... | collective-permute-start | bytes 1572872 | tf_op jit(solution)/shard_map/ppermute | solution.py:24
  71.4 31.3 %collective-permute-start.10 = (bf16[256,1024]{1,0:T(8,128)(2,1)S(1)}, bf16[256,1024]{1,0:T(8,128)(2,1)S(1)}, u32[]{:S(2)}, u32[]{:S(2)}) collective-permute-start(bf16[256,1024]{1,0:T(8,128)(2,1)S(1)} %get-tuple-element.31), channel_id=1, source_target_pairs={{0,8},{4,12},{8,0},{12,4},{16,24},{20,28},{24,16},{28,20},{1,9},{5... | collective-permute-start | bytes 1572872 | tf_op jit(solution)/shard_map/ppermute | solution.py:24
  71.4 32.5 %collective-permute-start.11 = (bf16[256,1024]{1,0:T(8,128)(2,1)S(1)}, bf16[256,1024]{1,0:T(8,128)(2,1)S(1)}, u32[]{:S(2)}, u32[]{:S(2)}) collective-permute-start(bf16[256,1024]{1,0:T(8,128)(2,1)S(1)} %get-tuple-element.32), channel_id=1, source_target_pairs={{0,16},{4,20},{8,24},{12,28},{16,0},{20,4},{24,8},{28,12},{1,17},{... | collective-permute-start | bytes 1572872 | tf_op jit(solution)/shard_map/ppermute | solution.py:24

commit v6 on v5

--- a/solution.py
+++ b/solution.py
@@ -14,7 +14,7 @@
 N_PARTNER = 3
 N_OWN = KB - N_PARTNER
 LANES = 256
-UNROLL = 2
+UNROLL = 4
 PARTS = 2
 LOG2E = 1.4426950408889634
 

time: 129 us -> 120 us (0.930)
  Pallas kernels: 47.5 us -> 39.4 us
    pallas_call x2, Pallas kernels: 41.5 us -> 33.4 us  [attend(): pl.pallas_call(functools.partial(attend_body, unroll, len(own)), grid_spe...]
  transfers between devices with their start and end apart: 12 -> 12, of which waited for: 5 -> 5; matrix products, arithmetic and copies ran while one was open for 27% -> 29% of each run, Pallas kernels for 16% -> 14%
where the time goes in v6:
time: 120 us
  Pallas kernels  39.4 us (33%)
  matrix products  35.1 us (29%)
  waiting for transfers between devices  21.1 us (18%)
  starting transfers between devices  18.6 us (16%)
  local copies, waits for them, and re-layouts  3.24 us (3%)
  other arithmetic  2.01 us (2%)
    dot_general x13, matrix products, project(): jnp.dot(rows, weights, preferred_element_type=jnp.float32)  35.1 us
    pallas_call x2, Pallas kernels, attend(): pl.pallas_call(functools.partial(attend_body, unroll, len(own)), grid_spe...  33.4 us
    ppermute x12, waiting for transfers between devices, exchange(): return lax.ppermute(value, axis, pairs)  21.1 us
    ppermute x12, starting transfers between devices, exchange(): return lax.ppermute(value, axis, pairs)  18.6 us
    pallas_call x2, Pallas kernels, pick_blocks(): pl.pallas_call(pick_body, grid_spec=pltpu.PrefetchScalarGridSpec(num_scal...  6.03 us
    unnamed x20, local copies, waits for them, and re-layouts  2.59 us
  transfers between devices with their start and end apart: 12, of which 5 were waited for; matrix products, arithmetic and copies ran while one was open for 29% of the time, Pallas kernels for 14%

profile of v6, /device:TPU:0, one launch (start us, length us, event | category | flops | bytes accessed | tf_op | source)
XLA Modules:
  0.0 119.7 jit_solution(18381418011187611883)
XLA Ops:
  0.0 2.9 %collective-permute-start.4 = (bf16[512,1024]{1,0:T(8,128)(2,1)}, bf16[512,1024]{1,0:T(8,128)(2,1)}, u32[]{:S(2)}, u32[]{:S(2)}) collective-permute-start(bf16[512,1024]{1,0:T(8,128)(2,1)} %refs_0_.3), channel_id=1, source_target_pairs={{0,2},{1,3},{2,0},{3,1},{4,6},{5,7},{6,4},{7,5},{8,10},{9,11},{10,... | collective-permute-start | bytes 3145736 | tf_op jit(solution)/shard_map/ppermute | solution.py:24
  2.9 0.8 fusion.8
  3.7 2.7 %collective-permute-start.2 = (s32[8]{0:T(128)S(1)}, s32[8]{0:T(128)S(1)}, u32[]{:S(2)}, u32[]{:S(2)}) collective-permute-start(s32[8]{0:T(128)S(1)} %get-tuple-element.38), channel_id=1, source_target_pairs={{0,16},{4,20},{8,24},{12,28},{16,0},{20,4},{24,8},{28,12},{1,17},{... | collective-permute-start | bytes 104 | tf_op jit(solution)/shard_map/ppermute | solution.py:24
  6.4 1.5 %collective-permute-start = (s32[8]{0:T(128)S(1)}, s32[8]{0:T(128)S(1)}, u32[]{:S(2)}, u32[]{:S(2)}) collective-permute-start(s32[8]{0:T(128)S(1)} %get-tuple-element.37), channel_id=1, source_target_pairs={{0,4},{4,0},{8,12},{12,8},{16,20},{20,16},{24,28},{28,24},{1,5},{5... | collective-permute-start | bytes 104 | tf_op jit(solution)/shard_map/ppermute | solution.py:24
  7.9 1.6 %collective-permute-start.1 = (s32[8]{0:T(128)S(1)}, s32[8]{0:T(128)S(1)}, u32[]{:S(2)}, u32[]{:S(2)}) collective-permute-start(s32[8]{0:T(128)S(1)} %get-tuple-element.39), channel_id=1, source_target_pairs={{0,8},{4,12},{8,0},{12,4},{16,24},{20,28},{24,16},{28,20},{1,9},{5... | collective-permute-start | bytes 104 | tf_op jit(solution)/shard_map/ppermute | solution.py:24
  9.5 6.2 %convolution_convert_fusion.3.refs_0_.refs_4_ = bf16[512,2048]{1,0:T(8,128)(2,1)} fusion(bf16[512,1024]{1,0:T(8,128)(2,1)} %refs_0_.3, bf16[1024,3072]{1,0:T(8,128)(2,1)} %param.5), kind=kOutput, calls=%fused_computation.3 | convolution fusion | flops 2148532224 | bytes 7340032 | tf_op jit(solution)/shard_map/dot_general | solution.py:180
  15.7 10.7 %collective-permute-done.4.refs_2_ = bf16[512,1024]{1,0:T(8,128)(2,1)} collective-permute-done((bf16[512,1024]{1,0:T(8,128)(2,1)}, bf16[512,1024]{1,0:T(8,128)(2,1)}, u32[]{:S(2)}, u32[]{:S(2)}) %collective-permute-start.4) | collective-permute-done | bytes 1048608 | tf_op jit(solution)/shard_map/ppermute | solution.py:24
  26.8 2.5 %collective-permute-done.5.refs_3_ = bf16[512,1024]{1,0:T(8,128)(2,1)S(1)} collective-permute-done((bf16[512,1024]{1,0:T(8,128)(2,1)}, bf16[512,1024]{1,0:T(8,128)(2,1)S(1)}, u32[]{:S(2)}, u32[]{:S(2)}) %collective-permute-start.5) | collective-permute-done | bytes 1048608 | tf_op jit(solution)/shard_map/ppermute | solution.py:24
  29.3 3.4 %shard_map.46 = (bf16[256,1024]{1,0:T(8,128)(2,1)}, bf16[256,1024]{1,0:T(8,128)(2,1)S(1)}, bf16[256,1024]{1,0:T(8,128)(2,1)S(1)}) custom-call(s32[12]{0:T(128)S(1)} %pad_add_fusion.index_ref, bf16[512,1024]{1,0:T(8,128)(2,1)S(1)} %copy-done.1, bf16[512,1024]{1,0:T(8,128)(2,1)} %collective-permute-done.3.refs_1_, ...), custom_call_target="tpu_custom_call" | custom-call | bytes 3145728 | tf_op jit(solution)/shard_map/pallas_call | solution.py:68
  32.7 1.0 copy-done.2
  34.4 0.8 copy-done.6
  35.2 1.6 %collective-permute-start.6 = (bf16[256,1024]{1,0:T(8,128)(2,1)}, bf16[256,1024]{1,0:T(8,128)(2,1)}, u32[]{:S(2)}, u32[]{:S(2)}) collective-permute-start(bf16[256,1024]{1,0:T(8,128)(2,1)} %get-tuple-element.19), channel_id=1, source_target_pairs={{0,4},{4,0},{8,12},{12,8},{16,20},{20,16},{24,28},{28,24},{1,5},{5... | collective-permute-start | bytes 1572872 | tf_op jit(solution)/shard_map/ppermute | solution.py:24
  37.3 2.9 %fusion.2.q_ref = bf16[512,1024]{1,0:T(8,128)(2,1)S(1)} fusion(bf16[512,1024]{1,0:T(8,128)(2,1)S(1)} %copy-done.1, bf16[1024,3072]{1,0:T(8,128)(2,1)} %param.5), kind=kOutput, calls=%fused_computation.12 | convolution fusion | flops 1074266112 | bytes 4194304 | tf_op jit(solution)/shard_map/dot_general | solution.py:180
  40.3 1.6 %collective-permute-start.7 = (bf16[256,1024]{1,0:T(8,128)(2,1)S(1)}, bf16[256,1024]{1,0:T(8,128)(2,1)S(1)}, u32[]{:S(2)}, u32[]{:S(2)}) collective-permute-start(bf16[256,1024]{1,0:T(8,128)(2,1)S(1)} %copy-done.7), channel_id=1, source_target_pairs={{0,8},{4,12},{8,0},{12,4},{16,24},{20,28},{24,16},{28,20},{1,9},{5... | collective-permute-start | bytes 1572872 | tf_op jit(solution)/shard_map/ppermute | solution.py:24
  41.9 2.9 %collective-permute-start.8 = (bf16[256,1024]{1,0:T(8,128)(2,1)S(1)}, bf16[256,1024]{1,0:T(8,128)(2,1)S(1)}, u32[]{:S(2)}, u32[]{:S(2)}) collective-permute-start(bf16[256,1024]{1,0:T(8,128)(2,1)S(1)} %copy-done.5), channel_id=1, source_target_pairs={{0,16},{4,20},{8,24},{12,28},{16,0},{20,4},{24,8},{28,12},{1,17},{... | collective-permute-start | bytes 1572872 | tf_op jit(solution)/shard_map/ppermute | solution.py:24
  44.8 5.2 %collective-permute-done.6 = bf16[256,1024]{1,0:T(8,128)(2,1)} collective-permute-done((bf16[256,1024]{1,0:T(8,128)(2,1)}, bf16[256,1024]{1,0:T(8,128)(2,1)}, u32[]{:S(2)}, u32[]{:S(2)}) %collective-permute-start.6) | collective-permute-done | bytes 524320 | tf_op jit(solution)/shard_map/ppermute | solution.py:24
  50.0 6.2 %convolution_convert_fusion.2.refs_1_.refs_5_ = bf16[512,2048]{1,0:T(8,128)(2,1)} fusion(bf16[512,1024]{1,0:T(8,128)(2,1)} %collective-permute-done.3.refs_1_, bf16[1024,3072]{1,0:T(8,128)(2,1)} %param.5), kind=kOutput, calls=%fused_computation.2 | convolution fusion | flops 2148532224 | bytes 7340032 | tf_op jit(solution)/shard_map/dot_general | solution.py:180
  56.2 5.0 %convolution_convert_fusion.1.refs_2_.refs_6_ = bf16[512,2048]{1,0:T(8,128)(2,1)} fusion(bf16[512,1024]{1,0:T(8,128)(2,1)} %collective-permute-done.4.refs_2_, bf16[1024,3072]{1,0:T(8,128)(2,1)S(1)} %bitcast.22), kind=kOutput, calls=%fused_computation.1 | convolution fusion | flops 2148532224 | bytes 7340032 | tf_op jit(solution)/shard_map/dot_general | solution.py:180
  61.2 3.7 %convolution_convert_fusion.refs_3_.refs_7_ = bf16[512,2048]{1,0:T(8,128)(2,1)} fusion(bf16[512,1024]{1,0:T(8,128)(2,1)S(1)} %copy-done.3, bf16[1024,3072]{1,0:T(8,128)(2,1)S(1)} %bitcast.22), kind=kOutput, calls=%fused_computation | convolution fusion | flops 2148532224 | bytes 7340032 | tf_op jit(solution)/shard_map/dot_general | solution.py:180
  65.5 2.2 %collective-permute-done.8 = bf16[256,1024]{1,0:T(8,128)(2,1)S(1)} collective-permute-done((bf16[256,1024]{1,0:T(8,128)(2,1)S(1)}, bf16[256,1024]{1,0:T(8,128)(2,1)S(1)}, u32[]{:S(2)}, u32[]{:S(2)}) %collective-permute-start.8) | collective-permute-done | bytes 524320 | tf_op jit(solution)/shard_map/ppermute | solution.py:24
  67.7 2.7 %shard_map.48 = (bf16[256,1024]{1,0:T(8,128)(2,1)S(1)}, bf16[256,1024]{1,0:T(8,128)(2,1)S(1)}, bf16[256,1024]{1,0:T(8,128)(2,1)S(1)}) custom-call(s32[12]{0:T(128)S(1)} %pad_add_fusion.1.index_ref, bf16[512,1024]{1,0:T(8,128)(2,1)S(1)} %copy-done.1, bf16[512,1024]{1,0:T(8,128)(2,1)} %collective-permute-done.3.refs_1_, ...), custom_call_target="tpu_custom_call" | custom-call | bytes 3145728 | tf_op jit(solution)/shard_map/pallas_call | solution.py:68
  70.3 0.8 collective-permute-start.9
  71.2 3.0 %collective-permute-start.11 = (bf16[256,1024]{1,0:T(8,128)(2,1)S(1)}, bf16[256,1024]{1,0:T(8,128)(2,1)S(1)}, u32[]{:S(2)}, u32[]{:S(2)}) collective-permute-start(bf16[256,1024]{1,0:T(8,128)(2,1)S(1)} %get-tuple-element.32), channel_id=1, source_target_pairs={{0,16},{4,20},{8,24},{12,28},{16,0},{20,4},{24,8},{28,12},{1,17},{... | collective-permute-start | bytes 1572872 | tf_op jit(solution)/shard_map/ppermute | solution.py:24
  74.1 2.3 %convolution_convert_fusion.9.refs_8_.refs_11_ = bf16[256,2048]{1,0:T(8,128)(2,1)S(1)} fusion(bf16[256,1024]{1,0:T(8,128)(2,1)} %collective-permute-done.6, bf16[1024,3072]{1,0:T(8,128)(2,1)S(1)} %bitcast.22), kind=kOutput, calls=%fused_computation.9 | convolution fusion | flops 1074266112 | bytes 5767168 | tf_op jit(solution)/shard_map/dot_general | solution.py:180
  76.4 1.3 %convolution_convert_fusion.8.refs_9_.refs_12_ = bf16[256,2048]{1,0:T(8,128)(2,1)S(1)} fusion(bf16[256,1024]{1,0:T(8,128)(2,1)S(1)} %collective-permute-done.7, bf16[1024,3072]{1,0:T(8,128)(2,1)S(1)} %bitcast.22), kind=kOutput, calls=%fused_computation.8 | convolution fusion | flops 1074266112 | bytes 5767168 | tf_op jit(solution)/shard_map/dot_general | solution.py:180
  77.7 1.3 %convolution_convert_fusion.7.refs_10_.refs_13_ = bf16[256,2048]{1,0:T(8,128)(2,1)S(1)} fusion(bf16[256,1024]{1,0:T(8,128)(2,1)S(1)} %collective-permute-done.8, bf16[1024,3072]{1,0:T(8,128)(2,1)S(1)} %bitcast.22), kind=kOutput, calls=%fused_computation.7 | convolution fusion | flops 1074266112 | bytes 5767168 | tf_op jit(solution)/shard_map/dot_general | solution.py:180
  79.0 16.7 %shard_map.47 = bf16[256,1024]{1,0:T(8,128)(2,1)S(1)} custom-call(s32[40]{0:T(128)S(1)} %reshape.6.index_ref, bf16[512,1024]{1,0:T(8,128)(2,1)S(1)} %fusion.2.q_ref, bf16[512,2048]{1,0:T(8,128)(2,1)} %convolution_convert_fusion.3.refs_0_.refs_4_, bf16[512,2048]{1,0:T(8,128)(2,1)} %convolution_convert_fusion.2.refs_1_.refs_5_, ...), custom_call_target="tpu_custom_call" | custom-call | flops 6979321856 | bytes 8388608 | tf_op jit(solution)/shard_map/pallas_call | solution.py:154
  96.4 2.3 %convolution_convert_fusion.6.refs_8_.refs_11_ = bf16[256,2048]{1,0:T(8,128)(2,1)S(1)} fusion(bf16[256,1024]{1,0:T(8,128)(2,1)} %collective-permute-done.9, bf16[1024,3072]{1,0:T(8,128)(2,1)S(1)} %bitcast.22), kind=kOutput, calls=%fused_computation.6 | convolution fusion | flops 1074266112 | bytes 5767168 | tf_op jit(solution)/shard_map/dot_general | solution.py:180
  98.7 1.3 %convolution_convert_fusion.5.refs_9_.refs_12_ = bf16[256,2048]{1,0:T(8,128)(2,1)S(1)} fusion(bf16[256,1024]{1,0:T(8,128)(2,1)S(1)} %collective-permute-done.10, bf16[1024,3072]{1,0:T(8,128)(2,1)S(1)} %bitcast.22), kind=kOutput, calls=%fused_computation.5 | convolution fusion | flops 1074266112 | bytes 5767168 | tf_op jit(solution)/shard_map/dot_general | solution.py:180
  100.0 1.3 %convolution_convert_fusion.4.refs_10_.refs_13_ = bf16[256,2048]{1,0:T(8,128)(2,1)S(1)} fusion(bf16[256,1024]{1,0:T(8,128)(2,1)S(1)} %collective-permute-done.11, bf16[1024,3072]{1,0:T(8,128)(2,1)S(1)} %bitcast.22), kind=kOutput, calls=%fused_computation.4 | convolution fusion | flops 1074266112 | bytes 5767168 | tf_op jit(solution)/shard_map/dot_general | solution.py:180
  101.2 16.7 %shard_map.49 = bf16[256,1024]{1,0:T(8,128)(2,1)S(1)} custom-call(s32[40]{0:T(128)S(1)} %reshape.7.index_ref, bf16[512,1024]{1,0:T(8,128)(2,1)S(1)} %fusion.2.q_ref, bf16[512,2048]{1,0:T(8,128)(2,1)} %convolution_convert_fusion.3.refs_0_.refs_4_, bf16[512,2048]{1,0:T(8,128)(2,1)} %convolution_convert_fusion.2.refs_1_.refs_5_, ...), custom_call_target="tpu_custom_call" | custom-call | flops 6979321856 | bytes 8388608 | tf_op jit(solution)/shard_map/pallas_call | solution.py:154
  118.6 1.0 pad_maximum_fusion
  (45 shorter events, 3.6 us)
Async XLA Ops:
  0.0 95.7 %copy-start = (bf16[1024,1024]{1,0:T(8,128)(2,1)S(1)}, bf16[1024,1024]{1,0:T(8,128)(2,1)}, u32[]{:S(2)}) copy-start(bf16[1024,1024]{1,0:T(8,128)(2,1)} %param.6) | copy-start | bytes 6291460
  0.0 26.4 %collective-permute-start.4 = (bf16[512,1024]{1,0:T(8,128)(2,1)}, bf16[512,1024]{1,0:T(8,128)(2,1)}, u32[]{:S(2)}, u32[]{:S(2)}) collective-permute-start(bf16[512,1024]{1,0:T(8,128)(2,1)} %refs_0_.3), channel_id=1, source_target_pairs={{0,2},{1,3},{2,0},{3,1},{4,6},{5,7},{6,4},{7,5},{8,10},{9,11},{10,... | collective-permute-start | bytes 3145736 | tf_op jit(solution)/shard_map/ppermute | solution.py:24
  2.9 23.8 %collective-permute-start.3 = (bf16[512,1024]{1,0:T(8,128)(2,1)}, bf16[512,1024]{1,0:T(8,128)(2,1)}, u32[]{:S(2)}, u32[]{:S(2)}) collective-permute-start(bf16[512,1024]{1,0:T(8,128)(2,1)} %refs_0_.3), channel_id=1, source_target_pairs={{0,1},{1,0},{2,3},{3,2},{4,5},{5,4},{6,7},{7,6},{8,9},{9,8},{10,11... | collective-permute-start | bytes 3145736 | tf_op jit(solution)/shard_map/ppermute | solution.py:24
  3.7 22.7 %collective-permute-start.2 = (s32[8]{0:T(128)S(1)}, s32[8]{0:T(128)S(1)}, u32[]{:S(2)}, u32[]{:S(2)}) collective-permute-start(s32[8]{0:T(128)S(1)} %get-tuple-element.38), channel_id=1, source_target_pairs={{0,16},{4,20},{8,24},{12,28},{16,0},{20,4},{24,8},{28,12},{1,17},{... | collective-permute-start | bytes 104 | tf_op jit(solution)/shard_map/ppermute | solution.py:24
  6.4 20.1 %collective-permute-start = (s32[8]{0:T(128)S(1)}, s32[8]{0:T(128)S(1)}, u32[]{:S(2)}, u32[]{:S(2)}) collective-permute-start(s32[8]{0:T(128)S(1)} %get-tuple-element.37), channel_id=1, source_target_pairs={{0,4},{4,0},{8,12},{12,8},{16,20},{20,16},{24,28},{28,24},{1,5},{5... | collective-permute-start | bytes 104 | tf_op jit(solution)/shard_map/ppermute | solution.py:24
  7.9 21.4 %copy-start.1 = (bf16[512,1024]{1,0:T(8,128)(2,1)S(1)}, bf16[512,1024]{1,0:T(8,128)(2,1)}, u32[]{:S(2)}) copy-start(bf16[512,1024]{1,0:T(8,128)(2,1)} %refs_0_.3) | copy-start | bytes 3145732
  7.9 18.6 %collective-permute-start.1 = (s32[8]{0:T(128)S(1)}, s32[8]{0:T(128)S(1)}, u32[]{:S(2)}, u32[]{:S(2)}) collective-permute-start(s32[8]{0:T(128)S(1)} %get-tuple-element.39), channel_id=1, source_target_pairs={{0,8},{4,12},{8,0},{12,4},{16,24},{20,28},{24,16},{28,20},{1,9},{5... | collective-permute-start | bytes 104 | tf_op jit(solution)/shard_map/ppermute | solution.py:24
  26.4 2.9 %collective-permute-start.5 = (bf16[512,1024]{1,0:T(8,128)(2,1)}, bf16[512,1024]{1,0:T(8,128)(2,1)S(1)}, u32[]{:S(2)}, u32[]{:S(2)}) collective-permute-start(bf16[512,1024]{1,0:T(8,128)(2,1)} %collective-permute-done.4.refs_2_), channel_id=1, source_target_pairs={{0,1},{1,0},{2,3},{3,2},{4,5},{5,4},{6,7},{7,6},{8,9},{9,8},{10,11... | collective-permute-start | bytes 3145736 | tf_op jit(solution)/shard_map/ppermute | solution.py:24
  32.7 1.0 copy-start.2
  33.6 0.8 copy-start.4
  34.4 0.8 copy-start.6
  35.2 14.8 %collective-permute-start.6 = (bf16[256,1024]{1,0:T(8,128)(2,1)}, bf16[256,1024]{1,0:T(8,128)(2,1)}, u32[]{:S(2)}, u32[]{:S(2)}) collective-permute-start(bf16[256,1024]{1,0:T(8,128)(2,1)} %get-tuple-element.19), channel_id=1, source_target_pairs={{0,4},{4,0},{8,12},{12,8},{16,20},{20,16},{24,28},{28,24},{1,5},{5... | collective-permute-start | bytes 1572872 | tf_op jit(solution)/shard_map/ppermute | solution.py:24
  37.3 3.0 %copy-start.7 = (bf16[256,1024]{1,0:T(8,128)(2,1)S(1)}, bf16[256,1024]{1,0:T(8,128)(2,1)}, u32[]{:S(2)}) copy-start(bf16[256,1024]{1,0:T(8,128)(2,1)} %copy-done.6) | copy-start | bytes 1572868
  37.3 4.6 %copy-start.5 = (bf16[256,1024]{1,0:T(8,128)(2,1)S(1)}, bf16[256,1024]{1,0:T(8,128)(2,1)}, u32[]{:S(2)}) copy-start(bf16[256,1024]{1,0:T(8,128)(2,1)} %copy-done.4) | copy-start | bytes 1572868
  40.3 25.2 %collective-permute-start.7 = (bf16[256,1024]{1,0:T(8,128)(2,1)S(1)}, bf16[256,1024]{1,0:T(8,128)(2,1)S(1)}, u32[]{:S(2)}, u32[]{:S(2)}) collective-permute-start(bf16[256,1024]{1,0:T(8,128)(2,1)S(1)} %copy-done.7), channel_id=1, source_target_pairs={{0,8},{4,12},{8,0},{12,4},{16,24},{20,28},{24,16},{28,20},{1,9},{5... | collective-permute-start | bytes 1572872 | tf_op jit(solution)/shard_map/ppermute | solution.py:24
  41.9 14.2 %slice-start = ((s8[6291456]{0:T(1024)(128)(4,1)}), s8[4194304]{0:T(1024)(128)(4,1)S(1)}, s32[]{:S(2)}) async-start(s8[6291456]{0:T(1024)(128)(4,1)} %bitcast.21), calls=%async_computation | async-start | bytes 8388608
  41.9 14.2 %slice-start.1 = ((s8[6291456]{0:T(1024)(128)(4,1)}), s8[2097152]{0:T(1024)(128)(4,1)S(1)}, s32[]{:S(2)}) async-start(s8[6291456]{0:T(1024)(128)(4,1)} %bitcast.21), calls=%async_computation.1 | async-start | bytes 4194304
  41.9 25.7 %collective-permute-start.8 = (bf16[256,1024]{1,0:T(8,128)(2,1)S(1)}, bf16[256,1024]{1,0:T(8,128)(2,1)S(1)}, u32[]{:S(2)}, u32[]{:S(2)}) collective-permute-start(bf16[256,1024]{1,0:T(8,128)(2,1)S(1)} %copy-done.5), channel_id=1, source_target_pairs={{0,16},{4,20},{8,24},{12,28},{16,0},{20,4},{24,8},{28,12},{1,17},{... | collective-permute-start | bytes 1572872 | tf_op jit(solution)/shard_map/ppermute | solution.py:24
  56.2 5.0 %copy-start.3 = (bf16[512,1024]{1,0:T(8,128)(2,1)S(1)}, bf16[512,1024]{1,0:T(8,128)(2,1)}, u32[]{:S(2)}) copy-start(bf16[512,1024]{1,0:T(8,128)(2,1)} %copy-done.2) | copy-start | bytes 3145732
  70.3 26.1 %collective-permute-start.9 = (bf16[256,1024]{1,0:T(8,128)(2,1)S(1)}, bf16[256,1024]{1,0:T(8,128)(2,1)}, u32[]{:S(2)}, u32[]{:S(2)}) collective-permute-start(bf16[256,1024]{1,0:T(8,128)(2,1)S(1)} %get-tuple-element.30), channel_id=1, source_target_pairs={{0,4},{4,0},{8,12},{12,8},{16,20},{20,16},{24,28},{28,24},{1,5},{5... | collective-permute-start | bytes 1572872 | tf_op jit(solution)/shard_map/ppermute | solution.py:24
  71.2 27.5 %collective-permute-start.10 = (bf16[256,1024]{1,0:T(8,128)(2,1)S(1)}, bf16[256,1024]{1,0:T(8,128)(2,1)S(1)}, u32[]{:S(2)}, u32[]{:S(2)}) collective-permute-start(bf16[256,1024]{1,0:T(8,128)(2,1)S(1)} %get-tuple-element.31), channel_id=1, source_target_pairs={{0,8},{4,12},{8,0},{12,4},{16,24},{20,28},{24,16},{28,20},{1,9},{5... | collective-permute-start | bytes 1572872 | tf_op jit(solution)/shard_map/ppermute | solution.py:24
  71.2 28.8 %collective-permute-start.11 = (bf16[256,1024]{1,0:T(8,128)(2,1)S(1)}, bf16[256,1024]{1,0:T(8,128)(2,1)S(1)}, u32[]{:S(2)}, u32[]{:S(2)}) collective-permute-start(bf16[256,1024]{1,0:T(8,128)(2,1)S(1)} %get-tuple-element.32), channel_id=1, source_target_pairs={{0,16},{4,20},{8,24},{12,28},{16,0},{20,4},{24,8},{28,12},{1,17},{... | collective-permute-start | bytes 1572872 | tf_op jit(solution)/shard_map/ppermute | solution.py:24
